TPU v7x, 128 devices: a whole 4x4x4 slice. The times are simulated.
128 devices in a mesh: row: 16 (over z, y_lo, core), col: 8 (over y_hi, x).
Axes of the slice: x: 4, y: 4 (y_hi: 2, y_lo: 2; y = y_hi * 2 + y_lo), z: 4, core: 2. Of those that a mesh axis runs over, the one named last changes fastest.
Arguments:
- latent: bfloat16 [512, 1024, 256], P('row', 'col'), may hold values from -20.2 to 20.2
- w_expand: bfloat16 [256, 1024], replicated, may hold values from -0.375 to 0.375
- w_depth: bfloat16 [3, 3, 1024], replicated, may hold values from -2 to 2
- squeeze_down: bfloat16 [1024, 64], replicated, may hold values from -0.75 to 0.75
- squeeze_up: bfloat16 [64, 1024], replicated, may hold values from -0.75 to 0.75
- w_project: bfloat16 [1024, 256], replicated, may hold values from -0.75 to 0.75
- norm_gain: float32 [2, 2, 256], replicated, may hold values from 0.1 to 1.9
- attend_in: bfloat16 [2, 256, 768], replicated, may hold values from -0.375 to 0.375
- attend_out: bfloat16 [2, 256, 256], replicated, may hold values from -0.375 to 0.375
- offset_bias: float32 [2, 8, 15, 15], replicated, may hold values from -4 to 310
- mixer_up: bfloat16 [2, 256, 1024], replicated, may hold values from -0.375 to 0.375
- mixer_down: bfloat16 [2, 1024, 256], replicated, may hold values from -0.1875 to 0.1875
Outputs:
- block_out: bfloat16 [512, 1024, 256], P('row', 'col')
All inputs are finite; a program needn't handle non-finite values.
Results may differ from a plain program's by a relative error of at most 0.013.
Values may be sent and summed in bfloat16 or wider, within the bound.
A program may use at most 128 MiB of HBM per device.

v0:
```python
import math

import jax
import jax.numpy as jnp
from jax import lax
from jax.sharding import PartitionSpec as P

WIN = 8


epsilon = 1e-05


def padded_2(array, sides, width):
    for axis, dim in sides:
        peers, length = (lax.axis_size(axis), array.shape[dim])
        up = [(i, (i + 1) % peers) for i in range(peers - 1)]
        down = [(j, i) for i, j in up]
        last = lax.slice_in_dim(array, length - width, length, axis=dim)
        leading = lax.slice_in_dim(array, 0, width, axis=dim)
        before = lax.ppermute(last, axis, up)
        after = lax.ppermute(leading, axis, down)
        array = jnp.concatenate([before, array, after], axis=dim)
    return array


def gelu_tanh(values):
    return jax.nn.gelu(values, approximate=True)


def rounded(values):
    return lax.optimization_barrier(values.astype(jnp.bfloat16))


def layer_norm(cell_rows, gain_row):
    floats = cell_rows.astype(jnp.float32)
    centre = floats - jnp.mean(floats, axis=-1, keepdims=True)
    spread = jnp.mean(centre * centre, axis=-1, keepdims=True)
    return rounded(centre * lax.rsqrt(spread + epsilon) * gain_row)


def bias_matrix(offset_table):
    head_count, span_rows, span_cols = offset_table.shape
    window_side = (span_rows + 1) // 2
    cell_ids = jnp.arange(window_side * window_side)
    row_of = cell_ids // window_side
    col_of = cell_ids % window_side
    flat_index = (
        (row_of[:, None] - row_of[None, :] + window_side - 1) * span_cols
        + col_of[:, None]
        - col_of[None, :]
        + window_side
        - 1
    )
    selector = (
        flat_index.reshape(-1)[:, None] == jnp.arange(span_rows * span_cols)[None, :]
    ).astype(jnp.float32)
    picked = jnp.dot(
        selector,
        offset_table.reshape(head_count, span_rows * span_cols).T,
        precision=lax.Precision.HIGHEST,
    )
    return picked.T.reshape(head_count, window_side * window_side, window_side * window_side)


def attend(normed, weight_in, weight_out, offset_terms):
    window_count, cell_count, feature_count = normed.shape
    head_count = offset_terms.shape[0]
    head_size = feature_count // head_count
    packed = rounded(
        jnp.dot(normed.reshape(-1, feature_count), weight_in, preferred_element_type=jnp.float32)
    )
    packed = packed.reshape(window_count, cell_count, 3, head_count, head_size)
    scores = (
        jnp.einsum(
            "nqhd,nkhd->nhqk", packed[:, :, 0], packed[:, :, 1], preferred_element_type=jnp.float32
        )
        / math.sqrt(head_size)
        + offset_terms[None]
    )
    highest = jnp.max(scores, axis=-1, keepdims=True)
    raised = jnp.exp(scores - highest)
    weights = rounded(raised / jnp.sum(raised, axis=-1, keepdims=True))
    mixture = rounded(
        jnp.einsum("nhqk,nkhd->nqhd", weights, packed[:, :, 2], preferred_element_type=jnp.float32)
    )
    product = jnp.dot(
        mixture.reshape(-1, feature_count), weight_out, preferred_element_type=jnp.float32
    )
    return product.reshape(window_count, cell_count, feature_count)


def window_section(
    cell_rows, gain_pair, weight_in, weight_out, offset_terms, weight_up, weight_down
):
    feature_count = cell_rows.shape[-1]
    attended = rounded(
        cell_rows.astype(jnp.float32)
        + attend(layer_norm(cell_rows, gain_pair[0]), weight_in, weight_out, offset_terms)
    )
    normed = layer_norm(attended, gain_pair[1]).reshape(-1, feature_count)
    raised = rounded(gelu_tanh(jnp.dot(normed, weight_up, preferred_element_type=jnp.float32)))
    lowered = jnp.dot(raised, weight_down, preferred_element_type=jnp.float32).reshape(
        cell_rows.shape
    )
    return rounded(attended.astype(jnp.float32) + lowered)


def per_device(
    latent,
    w_expand,
    w_depth,
    squeeze_down,
    squeeze_up,
    w_project,
    norm_gain,
    attend_in,
    attend_out,
    offset_bias,
    mixer_up,
    mixer_down,
):
    tile_rows, tile_cols, features = latent.shape
    hidden_width = w_expand.shape[1]
    part_rows = latent.shape[0]
    part_cols = latent.shape[1]
    product = jnp.dot(latent.reshape(-1, features), w_expand, preferred_element_type=jnp.float32)
    padded = padded_2(
        rounded(gelu_tanh(product)).reshape(part_rows, part_cols, hidden_width),
        (("row", 0), ("col", 1)),
        1,
    )
    tap_weights = w_depth.astype(jnp.float32)
    depthwise = jnp.zeros((tile_rows, tile_cols, hidden_width), jnp.float32)
    for shift_row in range(3):
        for shift_col in range(3):
            depthwise = depthwise + tap_weights[shift_row, shift_col] * padded[
                shift_row : shift_row + tile_rows, shift_col : shift_col + tile_cols
            ].astype(jnp.float32)
    activated = gelu_tanh(depthwise)
    devices = lax.axis_size("row") * lax.axis_size("col")
    column_total = lax.psum(jnp.sum(activated, axis=(0, 1)), ("row", "col"))
    column_mean = column_total / (tile_rows * tile_cols * devices)
    gate_hidden = jax.nn.silu(
        jnp.dot(
            column_mean[None, :], squeeze_down.astype(jnp.float32), precision=lax.Precision.HIGHEST
        )
    )
    excite = jax.nn.sigmoid(
        jnp.dot(gate_hidden, squeeze_up.astype(jnp.float32), precision=lax.Precision.HIGHEST)
    )[0]
    gated_act = rounded(activated * excite)
    branch = jnp.dot(
        gated_act.reshape(-1, hidden_width), w_project, preferred_element_type=jnp.float32
    )
    conv_out = rounded(latent.reshape(-1, features).astype(jnp.float32) + branch).reshape(
        tile_rows, tile_cols, features
    )
    block_terms = bias_matrix(offset_bias[0])
    grid_terms = bias_matrix(offset_bias[1])
    window_cells = WIN * WIN
    window_rows = (
        conv_out.reshape(tile_rows // WIN, WIN, tile_cols // WIN, WIN, features)
        .transpose(0, 2, 1, 3, 4)
        .reshape(-1, window_cells, features)
    )
    blocked = window_section(
        window_rows,
        norm_gain[0],
        attend_in[0],
        attend_out[0],
        block_terms,
        mixer_up[0],
        mixer_down[0],
    )
    blocked = (
        blocked.reshape(tile_rows // WIN, tile_cols // WIN, WIN, WIN, features)
        .transpose(0, 2, 1, 3, 4)
        .reshape(tile_rows, tile_cols, features)
    )
    row_count = lax.axis_size("row")
    col_count = lax.axis_size("col")
    col_slots = WIN // col_count
    stride = tile_cols // col_slots
    owned_cols = stride // (row_count * col_count)
    row_groups = row_count // WIN
    outgoing = blocked.reshape(tile_rows, col_slots, row_count * col_count, owned_cols, features)
    incoming = lax.all_to_all(outgoing, ("row", "col"), split_axis=2, concat_axis=2, tiled=True)
    item_count = incoming.shape[0]
    grid_item_count = incoming.shape[0]
    unpacked = incoming.reshape(
        grid_item_count, col_slots, WIN, row_groups, col_count, owned_cols, features
    )
    grid_cells = unpacked.transpose(0, 3, 5, 2, 4, 1, 6).reshape(-1, window_cells, features)
    finished = window_section(
        grid_cells,
        norm_gain[1],
        attend_in[1],
        attend_out[1],
        grid_terms,
        mixer_up[1],
        mixer_down[1],
    )
    restored = finished.reshape(
        grid_item_count, row_groups, owned_cols, WIN, col_count, col_slots, features
    ).transpose(0, 5, 3, 1, 4, 2, 6)
    finished = restored.reshape(
        grid_item_count, col_slots, row_count, col_count, owned_cols, features
    ).reshape(item_count, col_slots, row_count * col_count, owned_cols, features)
    returned = lax.all_to_all(finished, ("row", "col"), split_axis=2, concat_axis=2, tiled=True)
    return returned.reshape(tile_rows, tile_cols, features)


def solution(mesh):
    in_specs = (P("row", "col", None), P(), P(), P(), P(), P(), P(), P(), P(), P(), P(), P())
    out_specs = P("row", "col", None)
    return jax.shard_map(
        per_device, mesh=mesh, in_specs=in_specs, out_specs=out_specs, check_vma=False
    )
```

profile of v0, /device:TPU:1, one launch (start us, length us, event | category | flops | bytes accessed | tf_op | source)
XLA Modules:
  0.0 503.5 jit_solution(937191019112666286)
XLA Ops:
  1.0 7.1 %fusion.9 = bf16[4096,1024]{1,0:T(8,128)(2,1)S(1)} fusion(bf16[4096,256]{1,0:T(8,128)(2,1)} %bitcast.191, bf16[256,1024]{1,0:T(8,128)(2,1)S(1)} %copy-done), kind=kOutput, calls=%fused_computation.13 | convolution fusion | flops 2185232384 | bytes 11010048 | tf_op jit(solution)/shard_map/dot_general | solution.py:127
  8.2 3.3 copy-done.2
  11.6 4.6 collective-permute-start
  16.2 1.9 collective-permute-start.1
  18.4 2.6 convolution_bitcast_fusion.1
  21.0 3.2 collective-permute-done.1
  25.6 3.1 collective-permute-start.2
  30.9 3.7 collective-permute-done.3
  34.6 18.8 %maximum_maximum_fusion = (bf16[34,129,1024]{2,1,0:T(8,128)(2,1)}, bf16[34,129,1024]{2,1,0:T(8,128)(2,1)}) fusion(bf16[1,128,1024]{2,1,0:T(8,128)(2,1)S(1)} %collective-permute-done.1, bf16[32,128,1024]{2,1,0:T(8,128)(2,1)} %bitcast.154, bf16[1,128,1024]{2,1,0:T(8,128)(2,1)S(1)} %collective-permute-done, bf16[34,1,1024]{2,1,0:T(2,128)(2,1)S(1)} %collective-permute-done.2, ...), kind=kLoop, calls=%fused_computation.46 | loop fusion | flops 71860224 | bytes 27017216 | tf_op jit(solution)/shard_map/concatenate | solution.py:23
  53.3 37.6 %fusion.84 = (f32[1024]{0:T(1024)S(1)}, f32[32,128,1024]{2,1,0:T(8,128)}) fusion(bf16[34,129,1024]{2,1,0:T(8,128)(2,1)} %get-tuple-element.14, f32[1024]{0:T(1024)S(1)} %bitcast.184, bf16[1,128,1024]{2,1,0:T(8,128)(2,1)S(1)} %collective-permute-done.1, bf16[32,128,1024]{2,1,0:T(8,128)(2,1)} %bitcast.155, f32[1024]{0:T(1024)S(1)} %bitcast.183, ...), kind=kLoop, calls=%fused_computation.150 | loop fusion | flops 155188224 | bytes 76062720 | tf_op jit(solution)/shard_map/reduce_sum | solution.py:142
  90.9 72.1 %psum.7 = f32[1024]{0:T(1024)S(1)} all-reduce(f32[1024]{0:T(1024)S(1)} %get-tuple-element.5), channel_id=1, replica_groups=mesh['row'=16,'col'=8] {'row','col'}, use_global_device_ids=true, to_apply=%region_1.0 | all-reduce | flops 1024 | bytes 8192 | tf_op jit(solution)/shard_map/psum | solution.py:142
  163.5 7.3 %multiply_convert_fusion = bf16[32,128,1024]{2,1,0:T(8,128)(2,1)S(1)} fusion(f32[32,128,1024]{2,1,0:T(8,128)} %get-tuple-element.6, f32[1024]{0:T(1024)S(1)} %add_divide_fusion), kind=kLoop, calls=%fused_computation.43 | loop fusion | flops 8388608 | bytes 25169920 | tf_op jit(solution)/shard_map/convert_element_type | solution.py:32
  170.9 2.7 fusion.39
  173.6 2.4 convert_bitcast_fusion.1
  178.8 4.9 copy.82
  183.9 2.9 multiply_convert_fusion.2
  186.8 4.5 convolution_convert_fusion.1
  191.2 8.6 %copy.90 = bf16[4096,768]{0,1:T(8,128)(2,1)} copy(bf16[4096,768]{1,0:T(8,128)(2,1)} %convolution_convert_fusion.1) | data formatting | bytes 12582912 | tf_op jit(solution)/shard_map/optimization_barrier | solution.py:32
  199.8 17.9 %reshape.263 = bf16[64,64,3,8,32]{1,0,4,3,2:T(8,128)(2,1)} reshape(bf16[4096,768]{0,1:T(8,128)(2,1)} %copy.90) | data formatting | bytes 12582912 | tf_op jit(solution)/shard_map/reshape | solution.py:73
  217.7 7.5 %fusion.87 = (bf16[64,64,1,8,32]{1,0,4,3,2:T(8,128)(2,1)}, bf16[64,64,1,8,32]{1,0,4,3,2:T(8,128)(2,1)S(1)}, bf16[64,64,1,8,32]{1,0,4,3,2:T(8,128)(2,1)S(1)}) fusion(bf16[64,64,3,8,32]{1,0,4,3,2:T(8,128)(2,1)} %reshape.263), kind=kLoop, calls=%fused_computation.152 | loop fusion | bytes 12582912 | tf_op jit(solution)/shard_map/slice | solution.py:85
  225.3 21.6 %fusion.54 = f32[64,8,64,64]{2,3,1,0:T(8,128)} fusion(bf16[64,64,1,8,32]{1,0,4,3,2:T(8,128)(2,1)S(1)} %get-tuple-element.12, bf16[64,64,1,8,32]{1,0,4,3,2:T(8,128)(2,1)S(1)} %get-tuple-element.11), kind=kOutput, calls=%fused_computation.84 | convolution fusion | flops 134217728 | bytes 12582912 | tf_op jit(solution)/shard_map/nqhd,nkhd->nhqk/dot_general | solution.py:75
  246.9 17.7 %fusion.92 = (f32[64,8,64]{2,1,0:T(8,128)S(1)}, f32[64,8,64,64]{2,3,1,0:T(8,128)}) fusion(f32[64,8,64,64]{2,3,1,0:T(8,128)} %fusion.54, f32[8,64,64]{1,2,0:T(8,128)S(1)} %copy.95), kind=kOutput, calls=%fused_computation.157 | output fusion | flops 12582975 | bytes 17039360 | tf_op jit(solution)/shard_map/sub | solution.py:82
  264.6 7.5 %divide_convert_fusion.1 = bf16[64,8,64,64]{2,3,1,0:T(8,128)(2,1)S(1)} fusion(f32[64,8,64,64]{2,3,1,0:T(8,128)} %get-tuple-element.37, f32[64,8,64]{2,1,0:T(8,128)S(1)} %get-tuple-element.36), kind=kLoop, calls=%fused_computation.40 | loop fusion | flops 4194304 | bytes 12713984 | tf_op jit(solution)/shard_map/convert_element_type | solution.py:32
  272.1 10.7 %convert_bitcast_fusion.3 = bf16[64,64,8,32]{1,3,2,0:T(8,128)(2,1)} fusion(bf16[64,8,64,64]{2,3,1,0:T(8,128)(2,1)S(1)} %divide_convert_fusion.1, bf16[64,64,1,8,32]{1,0,4,3,2:T(8,128)(2,1)S(1)} %copy-done.5), kind=kOutput, calls=%fused_computation.95 | convolution fusion | flops 135266304 | bytes 8388608 | tf_op jit(solution)/shard_map/nhqk,nkhd->nqhd/dot_general | solution.py:85
  282.8 3.6 add_convert_fusion.1
  289.9 5.8 %fusion.24 = bf16[4096,1024]{1,0:T(8,128)(2,1)S(1)} fusion(bf16[4096,256]{1,0:T(8,128)(2,1)S(1)} %bitcast.172, bf16[2,256,1024]{2,1,0:T(8,128)(2,1)S(1)} %copy-done.16), kind=kOutput, calls=%fused_computation.28 | convolution fusion | flops 2185232384 | bytes 11010048 | tf_op jit(solution)/shard_map/dot_general | solution.py:102
  295.7 2.7 fusion.50
  298.6 2.5 copy.99
  301.2 6.4 %all-to-all-start = ((bf16[32,1,128,1,256]{4,0,3,1,2:T(8,128)(2,1)}), bf16[32,1,128,1,256]{4,0,3,1,2:T(8,128)(2,1)}, u32[]{:S(2)}, u32[]{:S(2)}) async-start(bf16[32,1,128,1,256]{4,0,3,1,2:T(8,128)(2,1)} %copy.99), calls=%async_computation | async-start | bytes 4194304 | tf_op jit(solution)/shard_map/all_to_all | solution.py:188
  307.7 2.6 convolution_bitcast_fusion
  310.5 26.8 %all-to-all-done = bf16[32,1,128,1,256]{4,0,3,1,2:T(8,128)(2,1)} async-done(((bf16[32,1,128,1,256]{4,0,3,1,2:T(8,128)(2,1)}), bf16[32,1,128,1,256]{4,0,3,1,2:T(8,128)(2,1)}, u32[]{:S(2)}, u32[]{:S(2)}) %all-to-all-start) | async-done | bytes 2097184 | tf_op jit(solution)/shard_map/all_to_all | solution.py:188
  337.3 4.8 fusion.88
  343.6 1.5 multiply_reduce_fusion
  345.6 4.9 copy.101
  350.6 2.9 multiply_convert_fusion.1
  353.5 4.5 convolution_convert_fusion
  358.0 8.6 %copy.107 = bf16[4096,768]{0,1:T(8,128)(2,1)} copy(bf16[4096,768]{1,0:T(8,128)(2,1)} %convolution_convert_fusion) | data formatting | bytes 12582912 | tf_op jit(solution)/shard_map/optimization_barrier | solution.py:32
  366.6 17.9 %reshape.267 = bf16[64,64,3,8,32]{1,0,4,3,2:T(8,128)(2,1)} reshape(bf16[4096,768]{0,1:T(8,128)(2,1)} %copy.107) | data formatting | bytes 12582912 | tf_op jit(solution)/shard_map/reshape | solution.py:73
  384.5 7.5 %fusion.86 = (bf16[64,64,1,8,32]{1,0,4,3,2:T(8,128)(2,1)}, bf16[64,64,1,8,32]{1,0,4,3,2:T(8,128)(2,1)S(1)}, bf16[64,64,1,8,32]{1,0,4,3,2:T(8,128)(2,1)S(1)}) fusion(bf16[64,64,3,8,32]{1,0,4,3,2:T(8,128)(2,1)} %reshape.267), kind=kLoop, calls=%fused_computation.151 | loop fusion | bytes 12582912 | tf_op jit(solution)/shard_map/slice | solution.py:85
  392.0 21.4 %fusion.52 = f32[64,8,64,64]{2,3,1,0:T(8,128)} fusion(bf16[64,64,1,8,32]{1,0,4,3,2:T(8,128)(2,1)S(1)} %get-tuple-element.9, bf16[64,64,1,8,32]{1,0,4,3,2:T(8,128)(2,1)S(1)} %get-tuple-element.8), kind=kOutput, calls=%fused_computation.79 | convolution fusion | flops 134217728 | bytes 12582912 | tf_op jit(solution)/shard_map/nqhd,nkhd->nhqk/dot_general | solution.py:75
  413.4 17.8 %fusion.93 = (f32[64,8,64]{2,1,0:T(8,128)S(1)}, f32[64,8,64,64]{2,3,1,0:T(8,128)}) fusion(f32[64,8,64,64]{2,3,1,0:T(8,128)} %fusion.52, f32[8,64,64]{1,2,0:T(8,128)S(1)} %copy.112), kind=kOutput, calls=%fused_computation.158 | output fusion | flops 12582975 | bytes 17039360 | tf_op jit(solution)/shard_map/sub | solution.py:82
  431.2 7.5 %divide_convert_fusion = bf16[64,8,64,64]{2,3,1,0:T(8,128)(2,1)S(1)} fusion(f32[64,8,64,64]{2,3,1,0:T(8,128)} %get-tuple-element.39, f32[64,8,64]{2,1,0:T(8,128)S(1)} %get-tuple-element.38), kind=kLoop, calls=%fused_computation.37 | loop fusion | flops 4194304 | bytes 12713984 | tf_op jit(solution)/shard_map/convert_element_type | solution.py:32
  438.6 10.7 %convert_bitcast_fusion.2 = bf16[64,64,8,32]{1,3,2,0:T(8,128)(2,1)} fusion(bf16[64,8,64,64]{2,3,1,0:T(8,128)(2,1)S(1)} %divide_convert_fusion, bf16[64,64,1,8,32]{1,0,4,3,2:T(8,128)(2,1)S(1)} %copy-done.6), kind=kOutput, calls=%fused_computation.91 | convolution fusion | flops 135266304 | bytes 8388608 | tf_op jit(solution)/shard_map/nhqk,nkhd->nqhd/dot_general | solution.py:85
  449.3 3.6 add_convert_fusion
  456.5 5.8 %fusion.32 = bf16[4096,1024]{1,0:T(8,128)(2,1)S(1)} fusion(bf16[4096,256]{1,0:T(8,128)(2,1)S(1)} %bitcast.173, bf16[2,256,1024]{2,1,0:T(8,128)(2,1)S(1)} %copy-done.17), kind=kOutput, calls=%fused_computation.36 | convolution fusion | flops 2185232384 | bytes 11010048 | tf_op jit(solution)/shard_map/dot_general | solution.py:102
  462.3 2.7 fusion.51
  466.2 34.4 %all_to_all.10 = bf16[32,1,128,1,256]{4,0,3,1,2:T(8,128)(2,1)S(1)} all-to-all(bf16[32,1,128,1,256]{4,0,3,1,2:T(8,128)(2,1)S(1)} %bitcast.170), channel_id=1, replica_groups=mesh['row'=16,'col'=8] {'row','col'}, dimensions={2} | all-to-all | bytes 4194304 | tf_op jit(solution)/shard_map/all_to_all | solution.py:210
  500.6 2.5 copy.116
  (101 shorter events, 19.0 us)
Async XLA Ops:
  0.0 1.0 copy-start
  1.0 17.1 %copy-start.12 = (bf16[3,3,1024]{2,1,0:T(4,128)(2,1)S(1)}, bf16[3,3,1024]{2,1,0:T(4,128)(2,1)}, u32[]{:S(2)}) copy-start(bf16[3,3,1024]{2,1,0:T(4,128)(2,1)} %param.14) | copy-start | bytes 55300
  1.0 17.1 %copy-start.11 = (f32[2,8,15,15]{3,1,2,0:T(8,128)S(1)}, f32[2,8,15,15]{3,1,2,0:T(8,128)}, u32[]{:S(2)}) copy-start(f32[2,8,15,15]{3,1,2,0:T(8,128)} %param.21) | copy-start | bytes 43204
  8.2 3.3 copy-start.2
  11.5 18.6 %copy-start.14 = (f32[2,2,256]{2,1,0:T(2,128)S(1)}, f32[2,2,256]{2,1,0:T(2,128)}, u32[]{:S(2)}) copy-start(f32[2,2,256]{2,1,0:T(2,128)} %param.18) | copy-start | bytes 12292
  11.6 9.5 %collective-permute-start = (bf16[1,128,1024]{2,1,0:T(8,128)(2,1)S(1)}, bf16[1,128,1024]{2,1,0:T(8,128)(2,1)S(1)}, u32[]{:S(2)}, u32[]{:S(2)}) collective-permute-start(bf16[1,128,1024]{2,1,0:T(8,128)(2,1)S(1)} %get-tuple-element.17), channel_id=1, source_target_pairs={{0,8},{8,16},{16,24},{24,32},{32,40},{40,48},{48,56},{56,64},{64,7... | collective-permute-start | bytes 786440 | tf_op jit(solution)/shard_map/ppermute | solution.py:21
  16.2 8.1 %collective-permute-start.1 = (bf16[1,128,1024]{2,1,0:T(8,128)(2,1)S(1)}, bf16[1,128,1024]{2,1,0:T(8,128)(2,1)S(1)}, u32[]{:S(2)}, u32[]{:S(2)}) collective-permute-start(bf16[1,128,1024]{2,1,0:T(8,128)(2,1)S(1)} %get-tuple-element.18), channel_id=1, source_target_pairs={{8,0},{16,8},{24,16},{32,24},{40,32},{48,40},{56,48},{64,56},{72,6... | collective-permute-start | bytes 786440 | tf_op jit(solution)/shard_map/ppermute | solution.py:22
  25.6 5.2 %collective-permute-start.2 = (bf16[34,1,1024]{2,1,0:T(2,128)(2,1)S(1)}, bf16[34,1,1024]{2,1,0:T(2,128)(2,1)S(1)}, u32[]{:S(2)}, u32[]{:S(2)}) collective-permute-start(bf16[34,1,1024]{2,1,0:T(2,128)(2,1)S(1)} %get-tuple-element.15), channel_id=1, source_target_pairs={{0,1},{1,2},{2,3},{3,4},{4,5},{5,6},{6,7},{8,9},{9,10},{10,11},{11... | collective-permute-start | bytes 208904 | tf_op jit(solution)/shard_map/ppermute | solution.py:21
  28.8 5.8 %collective-permute-start.3 = (bf16[34,1,1024]{2,1,0:T(2,128)(2,1)S(1)}, bf16[34,1,1024]{2,1,0:T(2,128)(2,1)S(1)}, u32[]{:S(2)}, u32[]{:S(2)}) collective-permute-start(bf16[34,1,1024]{2,1,0:T(2,128)(2,1)S(1)} %get-tuple-element.16), channel_id=1, source_target_pairs={{1,0},{2,1},{3,2},{4,3},{5,4},{6,5},{7,6},{9,8},{10,9},{11,10},{12... | collective-permute-start | bytes 208904 | tf_op jit(solution)/shard_map/ppermute | solution.py:22
  53.3 109.7 %copy-start.21 = (bf16[1024,64]{0,1:T(8,128)(2,1)S(1)}, bf16[1024,64]{0,1:T(8,128)(2,1)}, u32[]{:S(2)}) copy-start(bf16[1024,64]{0,1:T(8,128)(2,1)} %param.15) | copy-start | bytes 393220
  53.3 109.9 %copy-start.10 = (bf16[64,1024]{1,0:T(8,128)(2,1)S(1)}, bf16[64,1024]{1,0:T(8,128)(2,1)}, u32[]{:S(2)}) copy-start(bf16[64,1024]{1,0:T(8,128)(2,1)} %param.16) | copy-start | bytes 393220
  163.5 7.4 %copy-start.15 = (bf16[32,128,256]{2,1,0:T(8,128)(2,1)S(1)}, bf16[32,128,256]{2,1,0:T(8,128)(2,1)}, u32[]{:S(2)}) copy-start(bf16[32,128,256]{2,1,0:T(8,128)(2,1)} %param.12) | copy-start | bytes 6291460
  163.5 7.4 %copy-start.20 = (bf16[1024,256]{1,0:T(8,128)(2,1)S(1)}, bf16[1024,256]{1,0:T(8,128)(2,1)}, u32[]{:S(2)}) copy-start(bf16[1024,256]{1,0:T(8,128)(2,1)} %param.17) | copy-start | bytes 1572868
  178.3 8.4 %copy-start.7 = (bf16[2,256,768]{2,1,0:T(8,128)(2,1)S(1)}, bf16[2,256,768]{2,1,0:T(8,128)(2,1)}, u32[]{:S(2)}) copy-start(bf16[2,256,768]{2,1,0:T(8,128)(2,1)} %param.19) | copy-start | bytes 2359300
  264.6 7.5 %copy-start.5 = (bf16[64,64,1,8,32]{1,0,4,3,2:T(8,128)(2,1)S(1)}, bf16[64,64,1,8,32]{1,0,4,3,2:T(8,128)(2,1)}, u32[]{:S(2)}) copy-start(bf16[64,64,1,8,32]{1,0,4,3,2:T(8,128)(2,1)} %get-tuple-element.10) | copy-start | bytes 6291460
  272.1 10.7 %copy-start.3 = (f32[4,16,8,8,256]{4,3,2,1,0:T(8,128)S(1)}, f32[4,16,8,8,256]{4,3,2,1,0:T(8,128)}, u32[]{:S(2)}) copy-start(f32[4,16,8,8,256]{4,3,2,1,0:T(8,128)} %copy.82) | copy-start | bytes 12582916
  272.1 10.7 %copy-start.9 = (bf16[2,256,256]{2,1,0:T(8,128)(2,1)S(1)}, bf16[2,256,256]{2,1,0:T(8,128)(2,1)}, u32[]{:S(2)}) copy-start(bf16[2,256,256]{2,1,0:T(8,128)(2,1)} %param.20) | copy-start | bytes 786436
  282.8 7.1 %copy-start.16 = (bf16[2,256,1024]{2,1,0:T(8,128)(2,1)S(1)}, bf16[2,256,1024]{2,1,0:T(8,128)(2,1)}, u32[]{:S(2)}) copy-start(bf16[2,256,1024]{2,1,0:T(8,128)(2,1)} %param.22) | copy-start | bytes 3145732
  289.9 5.8 %copy-start.18 = (bf16[2,1024,256]{2,1,0:T(8,128)(2,1)S(1)}, bf16[2,1024,256]{2,1,0:T(8,128)(2,1)}, u32[]{:S(2)}) copy-start(bf16[2,1024,256]{2,1,0:T(8,128)(2,1)} %param.23) | copy-start | bytes 3145732
  301.2 36.1 %all-to-all-start = ((bf16[32,1,128,1,256]{4,0,3,1,2:T(8,128)(2,1)}), bf16[32,1,128,1,256]{4,0,3,1,2:T(8,128)(2,1)}, u32[]{:S(2)}, u32[]{:S(2)}) async-start(bf16[32,1,128,1,256]{4,0,3,1,2:T(8,128)(2,1)} %copy.99), calls=%async_computation | async-start | bytes 4194304 | tf_op jit(solution)/shard_map/all_to_all | solution.py:188
  345.1 8.4 %copy-start.8 = (bf16[2,256,768]{2,1,0:T(8,128)(2,1)S(1)}, bf16[2,256,768]{2,1,0:T(8,128)(2,1)}, u32[]{:S(2)}) copy-start(bf16[2,256,768]{2,1,0:T(8,128)(2,1)} %param.19) | copy-start | bytes 2359300
  431.2 7.5 %copy-start.6 = (bf16[64,64,1,8,32]{1,0,4,3,2:T(8,128)(2,1)S(1)}, bf16[64,64,1,8,32]{1,0,4,3,2:T(8,128)(2,1)}, u32[]{:S(2)}) copy-start(bf16[64,64,1,8,32]{1,0,4,3,2:T(8,128)(2,1)} %get-tuple-element.7) | copy-start | bytes 6291460
  438.6 10.7 %copy-start.4 = (f32[32,2,1,8,8,1,256]{6,4,3,1,0,5,2:T(8,128)S(1)}, f32[32,2,1,8,8,1,256]{6,4,3,1,0,5,2:T(8,128)}, u32[]{:S(2)}) copy-start(f32[32,2,1,8,8,1,256]{6,4,3,1,0,5,2:T(8,128)} %copy.101) | copy-start | bytes 12582916
  449.3 5.6 %copy-start.13 = (f32[1,1,256]{2,1,0:T(1,128)S(1)}, f32[1,1,256]{2,1,0:T(1,128)}, u32[]{:S(2)}) copy-start(f32[1,1,256]{2,1,0:T(1,128)} %get-tuple-element.32) | copy-start | bytes 3076
  449.3 7.1 %copy-start.17 = (bf16[2,256,1024]{2,1,0:T(8,128)(2,1)S(1)}, bf16[2,256,1024]{2,1,0:T(8,128)(2,1)}, u32[]{:S(2)}) copy-start(bf16[2,256,1024]{2,1,0:T(8,128)(2,1)} %param.22) | copy-start | bytes 3145732
  456.4 5.8 %copy-start.19 = (bf16[2,1024,256]{2,1,0:T(8,128)(2,1)S(1)}, bf16[2,1024,256]{2,1,0:T(8,128)(2,1)}, u32[]{:S(2)}) copy-start(bf16[2,1024,256]{2,1,0:T(8,128)(2,1)} %param.23) | copy-start | bytes 3145732
  462.3 40.8 %copy-start.1 = (bf16[256,1024]{1,0:T(8,128)(2,1)S(1)}, bf16[256,1024]{1,0:T(8,128)(2,1)}, u32[]{:S(2)}) copy-start(bf16[256,1024]{1,0:T(8,128)(2,1)} %param.13) | copy-start | bytes 1572868
where the time goes:
time: 512 us; the launch traced here: 504 us
  other arithmetic  140 us (27%)
  matrix products  113 us (22%)
  blocking collectives  107 us (21%)
  local copies, waits for them, and re-layouts  92.2 us (18%)
  waiting for transfers between devices  33.7 us (7%)
  starting transfers between devices  17.3 us (3%)
    psum x1, blocking collectives, per_device(): column_total = lax.psum(jnp.sum(activated, axis=(0, 1)), ('row', 'col'))  72.1 us
    dot_general x2, matrix products, attend(): jnp.einsum('nqhd,nkhd->nhqk', packed[:, :, 0], packed[:, :, 1], preferred...  43 us
    reduce_sum x1, other arithmetic, per_device(): column_total = lax.psum(jnp.sum(activated, axis=(0, 1)), ('row', 'col'))  37.6 us
    reshape x2, local copies, waits for them, and re-layouts, attend(): packed = packed.reshape(window_count, cell_count, 3, head_count, head_size)  35.8 us
    sub x2, other arithmetic, attend(): raised = jnp.exp(scores - highest)  35.5 us
    all_to_all x1, blocking collectives, per_device(): lax.all_to_all(finished, ('row', 'col'), split_axis=2, concat_axis=2, til...  34.4 us
    convert_element_type x7, other arithmetic, rounded(): return lax.optimization_barrier(values.astype(jnp.bfloat16))  30.9 us
    all_to_all x1, waiting for transfers between devices, per_device(): lax.all_to_all(outgoing, ('row', 'col'), split_axis=2, concat_axis=2, til...  26.8 us
  transfers between devices with their start and end apart: 5, of which 3 were waited for; matrix products, arithmetic and copies ran while one was open for 1% of the time, Pallas kernels for 0%

commit v1 on v0

v1 whole, which is shorter than its diff:
```python
import functools
import math

import jax
import jax.numpy as jnp
from jax import lax
from jax.experimental import pallas as pl
from jax.experimental.pallas import tpu as pltpu
from jax.sharding import PartitionSpec as P

MESH = pl.DeviceIdType.MESH
BF = jnp.bfloat16
F32 = jnp.float32
WIN = 8
CELLS = 64
EPSILON = 1e-05
LOG2E = 1.4426950408889634
ROWS, COLS = 16, 8
BANDS = 4
NT = (((1,), (1,)), ((), ()))


def dot(a, b):
    return jnp.dot(a, b, preferred_element_type=F32)


def dot_nt(a, b):
    return lax.dot_general(a, b, NT, preferred_element_type=F32)


def twice_gelu(v):
    c1 = jnp.asarray(0.7978845608, v.dtype)
    c2 = jnp.asarray(0.7978845608 * 0.044715, v.dtype)
    return v + v * jnp.tanh(v * (c1 + c2 * (v * v)))


def normalise(x, gain):
    mean = jnp.sum(x, axis=-1, keepdims=True) * (1.0 / 256)
    centre = x - mean
    var = jnp.sum(centre * centre, axis=-1, keepdims=True) * (1.0 / 256)
    return (centre * lax.rsqrt(var + EPSILON) * gain).astype(BF)


def put(ref, rows, value):
    ref[0, rows, :] = value[:, :128]
    ref[1, rows, :] = value[:, 128:]


def take(ref, start, count, stride):
    rows = pl.ds(start, count, stride=stride)
    return jnp.concatenate([ref[0, rows, :], ref[1, rows, :]], axis=1)


def front_kernel(
    latent, w_expand, taps, down, up_t, w_project,
    act_out, w_out,
    flat, lat, edge_l, edge_r, halo_l, halo_r, halo_t, halo_b, corners, hid, hid_edge, act,
    total, ar1, ar2, send_sems, recv_sems, ar_send, ar_recv, out_sems,
):
    row, col = lax.axis_index("row"), lax.axis_index("col")
    up, dn = lax.rem(row + ROWS - 1, ROWS), lax.rem(row + 1, ROWS)
    lf, rt = lax.rem(col + COLS - 1, COLS), lax.rem(col + 1, COLS)
    barrier = pltpu.get_barrier_semaphore()
    neighbours = ((row, lf), (row, rt), (up, col), (dn, col), (up, lf), (up, rt), (dn, lf), (dn, rt))
    for who in neighbours:
        pl.semaphore_signal(barrier, inc=1, device_id=who, device_id_type=MESH)

    def greet_row(o, c):
        pl.semaphore_signal(barrier, inc=1, device_id=(lax.rem(row + o, ROWS), col), device_id_type=MESH)
        return c

    def greet_col(o, c):
        pl.semaphore_signal(barrier, inc=1, device_id=(row, lax.rem(col + o, COLS)), device_id_type=MESH)
        return c

    lax.fori_loop(1, ROWS, greet_row, 0)
    lax.fori_loop(1, COLS, greet_col, 0)

    def spread(y, c):
        put(flat, pl.ds(pl.multiple_of(y * 128, 128), 128), latent[y].astype(F32))
        for v in range(8):
            lat[y, v] = take(flat, y * 128 + v, 16, 8).astype(BF)
        return c

    lax.fori_loop(0, 32, spread, 0)
    edge_l[...] = take(flat, 0, 32, 128).astype(BF)
    edge_r[...] = take(flat, 127, 32, 128).astype(BF)
    pl.semaphore_wait(barrier, 8 + ROWS - 1 + COLS - 1)
    first, last = pl.ds(0, 16), pl.ds(16, 16)
    moves = (
        (edge_l, halo_r, (row, lf)),
        (edge_r, halo_l, (row, rt)),
        (lat.at[0], halo_b, (up, col)),
        (lat.at[31], halo_t, (dn, col)),
        (edge_l.at[first], corners.at[3], (up, lf)),
        (edge_r.at[first], corners.at[2], (up, rt)),
        (edge_l.at[last], corners.at[1], (dn, lf)),
        (edge_r.at[last], corners.at[0], (dn, rt)),
    )
    copies = []
    for i, (src, dst, who) in enumerate(moves):
        copy = pltpu.make_async_remote_copy(
            src_ref=src, dst_ref=dst, send_sem=send_sems.at[i], recv_sem=recv_sems.at[i], device_id=who, device_id_type=MESH
        )
        copy.start()
        copies.append(copy)

    def expand(i, c):
        cells = lat[pl.ds(i * 4, 4)].reshape(512, 256)
        for t in range(4):
            part = pl.ds(t * 256, 256)
            h = twice_gelu(dot(cells, w_expand[:, part]).astype(BF))
            hid[pl.ds(1 + i * 4, 4), 1:9, :, part] = h.reshape(4, 8, 16, 256)
        return c

    lax.fori_loop(0, 8, expand, 0)
    for copy in copies:
        copy.wait()
    zero = jnp.zeros((), BF)
    top = jnp.where(row > 0, halo_t[...], zero).reshape(128, 256)
    bottom = jnp.where(row < ROWS - 1, halo_b[...], zero).reshape(128, 256)
    rows2 = jnp.concatenate([top, bottom], axis=0)
    left = jnp.concatenate([
        halo_l[...], jnp.where(row > 0, corners[0], zero), jnp.where(row < ROWS - 1, corners[2], zero)], axis=0)
    right = jnp.concatenate([
        halo_r[...], jnp.where(row > 0, corners[1], zero), jnp.where(row < ROWS - 1, corners[3], zero)], axis=0)
    left = jnp.where(col > 0, left, zero)
    right = jnp.where(col < COLS - 1, right, zero)
    sides = jnp.concatenate([left, right], axis=0)
    for t in range(4):
        part = pl.ds(t * 256, 256)
        h = twice_gelu(dot(rows2, w_expand[:, part]).astype(BF)).reshape(2, 8, 16, 256)
        hid[0, 1:9, :, part] = h[0]
        hid[33, 1:9, :, part] = h[1]
        hid_edge[:, part] = twice_gelu(dot(sides, w_expand[:, part]).astype(BF)).astype(F32)

    lane_n = lax.broadcasted_iota(jnp.int32, (16, 1024), 0)

    def wrap(y, c):
        place = jnp.where(y == 0, 47, jnp.where(y == 33, 48, y - 1))
        before = pltpu.roll(hid[y, 8].astype(F32), 1, 0)
        hid[y, 0] = jnp.where(lane_n == 0, hid_edge[pl.ds(place, 1), :], before).astype(BF)
        after = pltpu.roll(hid[y, 1].astype(F32), 15, 0)
        hid[y, 9] = jnp.where(lane_n == 15, hid_edge[pl.ds(place + 64, 1), :], after).astype(BF)
        return c

    lax.fori_loop(0, 34, wrap, 0)

    for t in range(8):
        part = pl.ds(t * 128, 128)
        weights = [taps[i, :, part] for i in range(9)]

        def depthwise(y, sums):
            acc = None
            for r in range(3):
                cells = hid[y + r, :, :, part]
                for s in range(3):
                    term = weights[r * 3 + s][None] * cells[s : s + 8]
                    acc = term if acc is None else acc + term
            a = twice_gelu(acc)
            act[y, :, :, part] = a
            b = a[:4] + a[4:]
            b = b[:2] + b[2:]
            return sums + (b[0] + b[1]).astype(F32)

        sums = lax.fori_loop(0, 32, depthwise, jnp.zeros((16, 128), F32))
        total[t : t + 1, :] = jnp.sum(sums, axis=0, keepdims=True)
        pltpu.make_async_copy(act.at[:, :, :, part], act_out.at[:, :, :, part], out_sems.at[t]).start()

    ar1[row] = total[...]

    def send_row(o, c):
        pltpu.make_async_remote_copy(
            src_ref=total, dst_ref=ar1.at[row], send_sem=ar_send.at[0], recv_sem=ar_recv.at[0],
            device_id=(lax.rem(row + o, ROWS), col), device_id_type=MESH).start()
        return c

    lax.fori_loop(1, ROWS, send_row, 0)
    rest = ar1.at[pl.ds(0, ROWS - 1)]
    pltpu.make_async_copy(rest, rest, ar_recv.at[0]).wait()
    pltpu.make_async_copy(rest, rest, ar_send.at[0]).wait()
    ar2[col] = jnp.sum(ar1[...], axis=0)

    def send_col(o, c):
        pltpu.make_async_remote_copy(
            src_ref=ar2.at[col], dst_ref=ar2.at[col], send_sem=ar_send.at[1], recv_sem=ar_recv.at[1],
            device_id=(row, lax.rem(col + o, COLS)), device_id_type=MESH).start()
        return c

    lax.fori_loop(1, COLS, send_col, 0)
    rest = ar2.at[pl.ds(0, COLS - 1)]
    pltpu.make_async_copy(rest, rest, ar_recv.at[1]).wait()
    pltpu.make_async_copy(rest, rest, ar_send.at[1]).wait()
    total[...] = jnp.sum(ar2[...], axis=0) * (0.5 / (512 * 1024))
    squeeze = jnp.concatenate([total[i : i + 1, :] for i in range(8)], axis=1)
    squeeze = jnp.broadcast_to(squeeze, (8, 1024))
    gate = jnp.dot(squeeze, down[...].astype(F32), precision=lax.Precision.HIGHEST, preferred_element_type=F32)
    gate = gate * jax.nn.sigmoid(gate)
    excite = jax.nn.sigmoid(jnp.sum(up_t[...].astype(F32) * gate[0:1, :], axis=1, keepdims=True))
    w_out[...] = (w_project[...].astype(F32) * (0.5 * excite)).astype(BF)
    for t in range(8):
        part = pl.ds(t * 128, 128)
        pltpu.make_async_copy(act.at[:, :, :, part], act_out.at[:, :, :, part], out_sems.at[t]).wait()


def front(latent, w_expand, taps, down, up_t, w_project):
    vmem = pl.BlockSpec(memory_space=pltpu.VMEM)
    return pl.pallas_call(
        front_kernel,
        out_shape=(jax.ShapeDtypeStruct((32, 8, 16, 1024), BF), jax.ShapeDtypeStruct((1024, 256), BF)),
        in_specs=[vmem] * 6,
        out_specs=(pl.BlockSpec(memory_space=pl.ANY), vmem),
        scratch_shapes=[
            pltpu.VMEM((2, 4096, 128), F32),
            pltpu.VMEM((32, 8, 16, 256), BF),
            pltpu.VMEM((32, 256), BF),
            pltpu.VMEM((32, 256), BF),
            pltpu.VMEM((32, 256), BF),
            pltpu.VMEM((32, 256), BF),
            pltpu.VMEM((8, 16, 256), BF),
            pltpu.VMEM((8, 16, 256), BF),
            pltpu.VMEM((4, 16, 256), BF),
            pltpu.VMEM((34, 10, 16, 1024), BF),
            pltpu.VMEM((128, 1024), F32),
            pltpu.VMEM((32, 8, 16, 1024), BF),
            pltpu.VMEM((8, 128), F32),
            pltpu.VMEM((ROWS, 8, 128), F32),
            pltpu.VMEM((COLS, 8, 128), F32),
            pltpu.SemaphoreType.DMA((8,)),
            pltpu.SemaphoreType.DMA((8,)),
            pltpu.SemaphoreType.DMA((2,)),
            pltpu.SemaphoreType.DMA((2,)),
            pltpu.SemaphoreType.DMA((8,)),
        ],
        compiler_params=pltpu.CompilerParams(collective_id=0, has_side_effects=True, vmem_limit_bytes=56 << 20),
        name="front",
    )(latent, w_expand, taps, down, up_t, w_project)


def attention_pair(q2, k2, vt2, bias, s):
    lane = lax.broadcasted_iota(jnp.int32, (64, 256), 1)
    lane_head = lax.rem(lane, 128) // 32
    lane_win = lax.broadcasted_iota(jnp.int32, (64, 128), 1) // 64
    zero = jnp.zeros((), BF)
    z = jnp.zeros((64, 128), BF)
    z32 = jnp.zeros((32, 128), BF)
    scale = LOG2E / math.sqrt(32)
    out = []
    for half in range(2):
        f = slice(half * 128, half * 128 + 128)
        qh, kh, vh = q2[:, f], k2[:, f], vt2[f, :]
        q_block = jnp.concatenate(
            [jnp.concatenate([qh[:64], z], axis=1), jnp.concatenate([z, qh[64:]], axis=1)], axis=0)
        k_both = jnp.concatenate([kh[:64], kh[64:]], axis=1)
        k_block = jnp.concatenate([jnp.where(lane_head == h, k_both, zero) for h in range(4)], axis=0)
        scores = dot_nt(k_block, q_block) * scale + bias[s, half]
        scores = scores.reshape(4, 64, 128)
        raised = jnp.exp2(scores - jnp.max(scores, axis=1, keepdims=True))
        inverse = 1.0 / jnp.sum(raised, axis=1, keepdims=True)
        weights = raised.astype(BF)
        rhs = jnp.concatenate(
            [jnp.where(lane_win == w, weights[h], zero) for h in range(4) for w in range(2)], axis=0)
        lhs = jnp.concatenate(
            [jnp.concatenate([vh[h * 32 : h * 32 + 32] if g == h else z32 for g in range(4)], axis=1) for h in range(4)],
            axis=0)
        mixed = dot(lhs, rhs).reshape(4, 32, 128) * inverse
        out.append(mixed.reshape(128, 128))
    return jnp.concatenate(out, axis=0)


def section_chunk(x, s, gains, w_qk, w_vt, w_o, w_up, w_down, bias):
    normed = normalise(x, gains[s, 0:1])
    qk = dot(normed, w_qk[s]).astype(BF)
    vt = dot_nt(w_vt[s], normed).astype(BF)
    mixes = []
    for p in range(2):
        r = slice(p * 128, p * 128 + 128)
        mixed = attention_pair(qk[r, :256], qk[r, 256:], vt[:, r], bias, s)
        mixes.append(mixed.T.astype(BF))
    mix = jnp.concatenate(mixes, axis=0)
    attended = (x + dot(mix, w_o[s])).astype(BF).astype(F32)
    normed = normalise(attended, gains[s, 1:2])
    lowered = jnp.zeros((256, 256), F32)
    for t in range(4):
        part = slice(t * 256, t * 256 + 256)
        up = twice_gelu(dot(normed, w_up[s, :, part]).astype(BF))
        lowered = lowered + dot(up, w_down[s, part, :])
    return attended + lowered


def sections_kernel(
    act, latent, w_project, gains, w_qk, w_vt, w_o, w_up, w_down, bias,
    returned,
    act_buf, conv, res, fwd_send, fwd_recv, back_send,
    act_sems, fs_sems, fr_sems, bs_sems, br_sems,
):
    row, col = lax.axis_index("row"), lax.axis_index("col")
    core, g = lax.rem(row, 2), row // 2
    me = g * 8 + col
    z, ylo, yhi, x = g // 2, lax.rem(g, 2), col // 4, lax.rem(col, 4)
    y = yhi * 2 + ylo
    barrier = pltpu.get_barrier_semaphore()

    def partner(o):
        dz = lax.rem(o, 4)
        x2 = lax.rem(x + o // 4 + dz, 4)
        y2 = lax.rem(y + o // 16 + dz, 4)
        z2 = lax.rem(z + dz, 4)
        g2, col2 = z2 * 2 + lax.rem(y2, 2), (y2 // 2) * 4 + x2
        return g2 * 8 + col2, (g2 * 2 + core, col2)

    def greet(o, c):
        _, who = partner(o)
        pl.semaphore_signal(barrier, inc=1, device_id=who, device_id_type=MESH)
        return c

    lax.fori_loop(1, 64, greet, 0)

    def fetch(k):
        slot = lax.rem(k, 2)
        return pltpu.make_async_copy(act.at[pl.ds(k * 8, 8)], act_buf.at[slot], act_sems.at[slot])

    def run_chunks(s, sink):
        def chunk(i, c):
            rows = pl.ds(pl.multiple_of(i * 256, 256), 256)
            sink(i, rows, section_chunk(res[rows, :], s, gains, w_qk, w_vt, w_o, w_up, w_down, bias))
            return c

        lax.fori_loop(0, 4, chunk, 0)

    fetch(0).start()
    pl.semaphore_wait(barrier, 63)

    def forward(k, c):
        @pl.when(k < BANDS - 1)
        def _():
            fetch(k + 1).start()

        fetch(k).wait()
        slot = lax.rem(k, 2)

        def project(i, c2):
            cells = act_buf[slot, pl.ds(i * 2, 2)].reshape(256, 1024)
            put(conv, pl.ds(pl.multiple_of(i * 256, 256), 256), dot(cells, w_project[...]))
            return c2

        lax.fori_loop(0, 4, project, 0)

        def regroup(n, c2):
            branch = take(conv, n, 64, 16)
            short = latent[pl.ds(k * 8, 8), pl.ds(pl.multiple_of(n // 2 * 16, 16), 16), :].astype(F32)
            short = jnp.where(lax.rem(n, 2) == 0, short[:, :8], short[:, 8:]).reshape(64, 256)
            res[pl.ds(pl.multiple_of(n * 64, 64), 64), :] = (branch + short).astype(BF).astype(F32)
            return c2

        lax.fori_loop(0, 16, regroup, 0)

        def sink(i, rows, value):
            fwd_send[k, pl.ds(i * 16, 16)] = value.astype(BF).reshape(16, 16, 256)

        run_chunks(0, sink)
        pltpu.make_async_copy(fwd_send.at[k, me], fwd_recv.at[k, me], fr_sems.at[k]).start()

        def send(o, c2):
            t, who = partner(o)
            pltpu.make_async_remote_copy(
                src_ref=fwd_send.at[k, t], dst_ref=fwd_recv.at[k, me], send_sem=fs_sems.at[k], recv_sem=fr_sems.at[k],
                device_id=who, device_id_type=MESH).start()
            return c2

        lax.fori_loop(1, 64, send, 0)
        return c

    lax.fori_loop(0, BANDS, forward, 0)

    def backward(k, c):
        pltpu.make_async_copy(fwd_recv.at[k], fwd_recv.at[k], fr_sems.at[k]).wait()

        def unpack(i, c2):
            put(conv, pl.ds(pl.multiple_of(i * 256, 256), 256), fwd_recv[k, pl.ds(i * 16, 16)].reshape(256, 256).astype(F32))
            return c2

        lax.fori_loop(0, 4, unpack, 0)

        def regroup(n, c2):
            res[pl.ds(pl.multiple_of(n * 64, 64), 64), :] = take(conv, n, 64, 16)
            return c2

        lax.fori_loop(0, 16, regroup, 0)

        def sink(i, rows, value):
            put(conv, rows, value)

        run_chunks(1, sink)

        def repack(t, c2):
            back_send[k, t] = take(conv, t, 16, 64).astype(BF)
            return c2

        lax.fori_loop(0, 64, repack, 0)
        pltpu.make_async_copy(back_send.at[k, me], returned.at[k, me], br_sems.at[k]).start()

        def send(o, c2):
            t, who = partner(o)
            pltpu.make_async_remote_copy(
                src_ref=back_send.at[k, t], dst_ref=returned.at[k, me], send_sem=bs_sems.at[k], recv_sem=br_sems.at[k],
                device_id=who, device_id_type=MESH).start()
            return c2

        lax.fori_loop(1, 64, send, 0)
        return c

    lax.fori_loop(0, BANDS, backward, 0)

    def finish(k, c):
        pltpu.make_async_copy(returned.at[k], returned.at[k], br_sems.at[k]).wait()
        for sems, buf in ((fs_sems, fwd_send), (bs_sems, back_send)):
            sent = buf.at[k, pl.ds(0, 63)]
            pltpu.make_async_copy(sent, sent, sems.at[k]).wait()
        return c

    lax.fori_loop(0, BANDS, finish, 0)


def sections(act, latent, w_project, gains, w_qk, w_vt, w_o, w_up, w_down, bias):
    vmem = pl.BlockSpec(memory_space=pltpu.VMEM)
    block = (BANDS, 64, 16, 256)
    return pl.pallas_call(
        sections_kernel,
        out_shape=jax.ShapeDtypeStruct(block, BF),
        in_specs=[pl.BlockSpec(memory_space=pl.ANY)] + [vmem] * 9,
        out_specs=pl.BlockSpec(memory_space=pl.ANY),
        scratch_shapes=[
            pltpu.VMEM((2, 8, 8, 16, 1024), BF),
            pltpu.VMEM((2, 1024, 128), F32),
            pltpu.VMEM((1024, 256), F32),
            pltpu.VMEM(block, BF),
            pltpu.VMEM(block, BF),
            pltpu.VMEM(block, BF),
            pltpu.SemaphoreType.DMA((2,)),
            pltpu.SemaphoreType.DMA((BANDS,)),
            pltpu.SemaphoreType.DMA((BANDS,)),
            pltpu.SemaphoreType.DMA((BANDS,)),
            pltpu.SemaphoreType.DMA((BANDS,)),
        ],
        compiler_params=pltpu.CompilerParams(collective_id=1, has_side_effects=True, vmem_limit_bytes=56 << 20),
        name="sections",
    )(act, latent, w_project, gains, w_qk, w_vt, w_o, w_up, w_down, bias)


def bias_tables(offset_bias):
    ids = jnp.arange(CELLS)
    r, c = ids // WIN, ids % WIN
    index = (r[None, :] - r[:, None] + 7) * 15 + c[None, :] - c[:, None] + 7
    selector = (jnp.arange(225)[:, None] == index.reshape(1, -1)).astype(F32)
    table = jnp.dot(offset_bias.reshape(16, 225) * LOG2E, selector, precision=lax.Precision.HIGHEST)
    table = table.reshape(2, 2, 256, 64)
    return jnp.concatenate([table, table], axis=-1)


def per_device(
    latent, w_expand, w_depth, squeeze_down, squeeze_up, w_project,
    norm_gain, attend_in, attend_out, offset_bias, mixer_up, mixer_down,
):
    taps = jnp.broadcast_to((w_depth * 0.5).reshape(9, 1, 1024), (9, 16, 1024))
    act, gated_project = front(latent, w_expand, taps, squeeze_down, squeeze_up.T, w_project)
    returned = sections(
        act, latent, gated_project, norm_gain,
        attend_in[:, :, :512], attend_in[:, :, 512:].transpose(0, 2, 1), attend_out, mixer_up, mixer_down * 0.5,
        bias_tables(offset_bias),
    )
    tiles = returned.reshape(BANDS, 16, WIN, WIN, 256).transpose(0, 2, 1, 3, 4)
    return tiles.reshape(32, 128, 256)


def solution(mesh):
    in_specs = (P("row", "col", None),) + (P(),) * 11
    return jax.shard_map(
        per_device, mesh=mesh, in_specs=in_specs, out_specs=P("row", "col", None), check_vma=False
    )
```

time: 512 us -> 169 us (0.33); the launches traced: 504 us -> 168 us
  Pallas kernels: 0 us -> 155 us
  other arithmetic: 140 us -> 4.06 us
  matrix products: 113 us -> 1.28 us
  blocking collectives: 107 us -> 0 us
  local copies, waits for them, and re-layouts: 92.2 us -> 7.78 us
  waiting for transfers between devices: 33.7 us -> 0 us
  starting transfers between devices: 17.3 us -> 0 us
    pallas_call x0 -> x2, Pallas kernels: none -> 155 us  [the longest x1 109 us: sections(): pl.pallas_call(sections_kernel, out_shape=jax.ShapeDtypeStruct(block, BF)...]
    dot_general x18 -> x1, matrix products: 113 us -> 1.28 us  [bias_tables(): jnp.dot(offset_bias.reshape(16, 225) * LOG2E, selector, precision=lax.Pre...]
    psum x1 -> x0, blocking collectives: 72.1 us -> none  [per_device(): column_total = lax.psum(jnp.sum(activated, axis=(0, 1)), ('row', 'col'))]
    reduce_sum x9 -> x0, other arithmetic: 45.8 us -> none  [the longest x1 37.6 us: per_device(): column_total = lax.psum(jnp.sum(activated, axis=(0, 1)), ('row', 'col'))]
    reshape x4 -> x1, local copies, waits for them, and re-layouts: 38.5 us -> 0.22 us  [bias_tables(): table = table.reshape(2, 2, 256, 64)]
    sub x3 -> x0, other arithmetic: 35.6 us -> none  [the longest x2 35.5 us: attend(): raised = jnp.exp(scores - highest)]
    all_to_all x1 -> x0, blocking collectives: 34.4 us -> none  [per_device(): lax.all_to_all(finished, ('row', 'col'), split_axis=2, concat_axis=2, til...]
    convert_element_type x8 -> x0, other arithmetic: 33.3 us -> none  [the longest x7 30.9 us: rounded(): return lax.optimization_barrier(values.astype(jnp.bfloat16))]
  transfers between devices with their start and end apart: 5 -> 0, of which waited for: 3 -> 0; matrix products, arithmetic and copies ran while one was open for 1% -> 0% of each run, Pallas kernels for 0% -> 0%
where the time goes in v1:
time: 169 us; the launch traced here: 168 us
  Pallas kernels  155 us (92%)
  local copies, waits for them, and re-layouts  7.78 us (5%)
  other arithmetic  4.06 us (2%)
    pallas_call x1, Pallas kernels, sections(): pl.pallas_call(sections_kernel, out_shape=jax.ShapeDtypeStruct(block, BF)...  109 us
    pallas_call x1, Pallas kernels, front(): pl.pallas_call(front_kernel, out_shape=(jax.ShapeDtypeStruct((32, 8, 16,...  46 us

profile of v1, /device:TPU:1, one launch (start us, length us, event | category | flops | bytes accessed | tf_op | source)
XLA Modules:
  0.0 168.4 jit_solution(9149061095707131434)
XLA Ops:
  0.0 0.0 slice-start
  0.0 0.0 copy-start.1
  0.0 0.0 copy-start
  0.0 0.0 copy-start.3
  0.0 0.0 copy-start.2
  0.0 1.0 broadcast_multiply_fusion.2
  1.0 0.1 subtract_add_fusion
  1.1 0.1 reshape.100
  1.2 0.9 broadcast_multiply_fusion.1
  2.1 0.1 mul.38
  2.3 1.3 fusion
  3.5 0.2 reshape.95
  3.8 1.0 pad_maximum_fusion.bias
  4.8 0.8 broadcast_in_dim.5.taps
  5.6 0.0 copy-done.2
  5.6 0.9 copy.18.down
  6.4 0.0 copy-done.3
  6.4 0.9 copy.17
  7.3 0.0 slice-done
  7.3 0.8 copy.22
  8.1 0.0 copy-done.1
  8.1 0.8 slice.6.w_qk
  8.9 0.0 copy-done
  8.9 1.1 broadcast_multiply_fusion.w_down
  10.0 46.0 %front.1 = (bf16[32,8,16,1024]{3,2,1,0:T(8,128)(2,1)}, bf16[1024,256]{1,0:T(8,128)(2,1)}) custom-call(bf16[32,128,256]{2,1,0:T(8,128)(2,1)} %latent.3, bf16[256,1024]{1,0:T(8,128)(2,1)} %w_expand.1, bf16[9,16,1024]{2,1,0:T(8,128)(2,1)} %broadcast_in_dim.5.taps, bf16[1024,64]{1,0:T(8,128)(2,1)} %copy.18.down, bf16[1024,64]{1,0:T(8,128)(2,1)} %bitcast.9, ...), custom_call_target="tpu_custom_call" | custom-call | tf_op jit(solution)/shard_map/front/pallas_call | solution.py:208
  56.0 109.2 %sections.1 = bf16[4,64,16,256]{3,2,1,0:T(8,128)(2,1)} custom-call(bf16[32,8,16,1024]{3,2,1,0:T(8,128)(2,1)} %get-tuple-element.7.act, bf16[32,128,256]{2,1,0:T(8,128)(2,1)} %latent.3, bf16[1024,256]{1,0:T(8,128)(2,1)} %get-tuple-element.8.w_project, f32[2,2,256]{2,1,0:T(2,128)} %gains.1, bf16[2,256,512]{2,1,0:T(8,128)(2,1)} %slice.6.w_qk, ...), custom_call_target="tpu_custom_call" | custom-call | tf_op jit(solution)/shard_map/sections/pallas_call | solution.py:428
  165.2 3.2 %copy.21 = bf16[4,8,16,8,256]{4,3,2,1,0:T(8,128)(2,1)} copy(bf16[4,8,16,8,256]{4,3,1,2,0:T(8,128)(2,1)} %bitcast.7) | data formatting | bytes 4194304 | tf_op jit(solution)/shard_map/transpose | solution.py:472
  (3 shorter events, 0.1 us)
Async XLA Ops:
  0.0 7.3 %slice-start = ((bf16[2,256,768]{2,1,0:T(8,128)(2,1)}), bf16[2,256,256]{2,1,0:T(8,128)(2,1)S(1)}, s32[]{:S(2)}) async-start(bf16[2,256,768]{2,1,0:T(8,128)(2,1)} %param.19), calls=%async_computation | async-start | bytes 524288 | tf_op jit(solution)/shard_map/slice | solution.py:469
  0.0 8.1 %copy-start.1 = (bf16[2,256,768]{2,1,0:T(8,128)(2,1)S(1)}, bf16[2,256,768]{2,1,0:T(8,128)(2,1)}, u32[]{:S(2)}) copy-start(bf16[2,256,768]{2,1,0:T(8,128)(2,1)} %param.19) | copy-start | bytes 2359300
  0.0 8.9 %copy-start = (bf16[2,1024,256]{2,1,0:T(8,128)(2,1)S(1)}, bf16[2,1024,256]{2,1,0:T(8,128)(2,1)}, u32[]{:S(2)}) copy-start(bf16[2,1024,256]{2,1,0:T(8,128)(2,1)} %param.23) | copy-start | bytes 3145732
  0.0 6.4 %copy-start.3 = (bf16[64,1024]{1,0:T(8,128)(2,1)S(1)}, bf16[64,1024]{1,0:T(8,128)(2,1)}, u32[]{:S(2)}) copy-start(bf16[64,1024]{1,0:T(8,128)(2,1)} %param.16) | copy-start | bytes 393220
  0.0 5.6 %copy-start.2 = (bf16[1024,64]{0,1:T(8,128)(2,1)S(1)}, bf16[1024,64]{0,1:T(8,128)(2,1)}, u32[]{:S(2)}) copy-start(bf16[1024,64]{0,1:T(8,128)(2,1)} %param.15) | copy-start | bytes 393220

commit v2 on v1

v2 whole, which is shorter than its diff:
```python
import math

import jax
import jax.numpy as jnp
from jax import lax
from jax.experimental import pallas as pl
from jax.experimental.pallas import tpu as pltpu
from jax.sharding import PartitionSpec as P

MESH = pl.DeviceIdType.MESH
BF = jnp.bfloat16
F32 = jnp.float32
EPSILON = 1e-05
LOG2E = 1.4426950408889634
ROWS, COLS = 16, 8
BANDS = 4
NT = (((1,), (1,)), ((), ()))


def dot(a, b):
    return jnp.dot(a, b, preferred_element_type=F32)


def dot_nt(a, b):
    return lax.dot_general(a, b, NT, preferred_element_type=F32)


def twice_gelu(v):
    c1 = jnp.asarray(0.7978845608, v.dtype)
    c2 = jnp.asarray(0.7978845608 * 0.044715, v.dtype)
    return v + v * jnp.tanh(v * (c1 + c2 * (v * v)))


def normalise(x, gain):
    mean = jnp.sum(x, axis=-1, keepdims=True) * (1.0 / 256)
    centre = x - mean
    var = jnp.sum(centre * centre, axis=-1, keepdims=True) * (1.0 / 256)
    return (centre * lax.rsqrt(var + EPSILON) * gain).astype(BF)


def put(ref, rows, value):
    ref[0, rows, :] = value[:, :128]
    ref[1, rows, :] = value[:, 128:]


def take(ref, start, count, stride):
    rows = pl.ds(start, count, stride=stride)
    return jnp.concatenate([ref[0, rows, :], ref[1, rows, :]], axis=1)


def lanes(value, t):
    return value[:, t * 128 : t * 128 + 128]


def attention_pair(q2, k2, vt2, bias, s):
    lane = lax.broadcasted_iota(jnp.int32, (64, 256), 1)
    lane_head = lax.rem(lane, 128) // 32
    first = lax.broadcasted_iota(jnp.int32, (32, 128), 1) < 64
    first_out = lax.broadcasted_iota(jnp.int32, (128, 128), 1) < 64
    zero = jnp.zeros((), BF)
    z = jnp.zeros((64, 128), BF)
    z32 = jnp.zeros((32, 128), BF)
    scale = LOG2E / math.sqrt(32)
    out = []
    for half in range(2):
        f = slice(half * 128, half * 128 + 128)
        qh, kh, vh = q2[:, f], k2[:, f], vt2[f, :]
        q_block = jnp.concatenate(
            [jnp.concatenate([qh[:64], z], axis=1), jnp.concatenate([z, qh[64:]], axis=1)], axis=0)
        k_both = jnp.concatenate([kh[:64], kh[64:]], axis=1)
        k_block = jnp.concatenate([jnp.where(lane_head == h, k_both, zero) for h in range(4)], axis=0)
        scores = dot_nt(k_block, q_block) * scale + bias[s, half]
        scores = scores.reshape(4, 64, 128)
        raised = jnp.exp2(scores - jnp.max(scores, axis=1, keepdims=True))
        inverse = 1.0 / jnp.sum(raised, axis=1, keepdims=True)
        weights = raised.astype(BF).reshape(256, 128)
        swapped = jnp.concatenate([vh[:, 64:], vh[:, :64]], axis=1)
        lhs = []
        for w in range(2):
            for h in range(4):
                source = (vh if h % 2 == w else swapped)[h * 32 : h * 32 + 32]
                kept = jnp.where(first, source, zero) if h % 2 == 0 else jnp.where(first, zero, source)
                lhs.append(jnp.concatenate([kept, z32] if h < 2 else [z32, kept], axis=1))
        mixed = dot(jnp.concatenate(lhs, axis=0), weights)
        mixed = jnp.where(first_out, mixed[:128], mixed[128:]).reshape(4, 32, 128) * inverse
        out.append(mixed.reshape(128, 128))
    return jnp.concatenate(out, axis=0)


def section_rows(x, s, gains, w_in, w_vt, w_o, w_up, w_down, bias):
    n = x.shape[0]
    normed = normalise(x, gains[s, 0:1])
    qk = dot(normed, w_in[s, :, :512]).astype(BF)
    vt = dot_nt(w_vt[s], normed).astype(BF)
    mixes = []
    for p in range(n // 128):
        r = slice(p * 128, p * 128 + 128)
        mixed = attention_pair(qk[r, :256], qk[r, 256:], vt[:, r], bias, s)
        mixes.append(mixed.T.astype(BF))
    mix = jnp.concatenate(mixes, axis=0)
    attended = (x + dot(mix, w_o[s])).astype(BF).astype(F32)
    normed = normalise(attended, gains[s, 1:2])
    up = [twice_gelu(dot(normed, w_up[s, :, t * 256 : t * 256 + 256]).astype(BF)) for t in range(4)]
    return attended + 0.5 * dot(jnp.concatenate(up, axis=1), w_down[s])


def bias_tables(offsets, flat, bias):
    pad = jnp.zeros((8, 113), F32)
    parts = []
    for s in range(2):
        for tile in range(2):
            acc = jnp.zeros((8, 128), F32)
            for r in range(tile * 8, min(tile * 8 + 8, 15)):
                row = jnp.concatenate([offsets[s, r] * LOG2E, pad], axis=1)
                shift = (r - tile * 8) * 16
                acc = acc + (pltpu.roll(row, shift, 1) if shift else row)
            parts.append(acc)
    table = jnp.concatenate(
        [jnp.concatenate(parts[:2], axis=1), jnp.concatenate(parts[2:], axis=1)], axis=0)
    high = table.astype(BF)
    rest = table - high.astype(F32)
    middle = rest.astype(BF)
    low = (rest - middle.astype(F32)).astype(BF)
    source = lax.broadcasted_iota(jnp.int32, (256, 128), 0)
    target = lax.broadcasted_iota(jnp.int32, (256, 128), 1)
    same_row = source // 16 == target // 8
    for key_col in range(8):
        pick = same_row & (lax.rem(source, 16) == lax.rem(target, 8) + (7 - key_col))
        pick = jnp.where(pick, 1.0, 0.0).astype(BF)
        flat[0, key_col * 16 : key_col * 16 + 16, :] = dot(high, pick) + dot(middle, pick) + dot(low, pick)
    left = lax.broadcasted_iota(jnp.int32, (8, 128), 1) < 64
    for s in range(2):
        for h in range(8):
            block = flat[0, pl.ds(s * 8 + h, 8, stride=16), :]
            for key_row in range(8):
                first = pltpu.roll(block, (128 - (7 - key_row) * 8) % 128, 1) if key_row < 7 else block
                both = jnp.where(left, first, pltpu.roll(first, 64, 1))
                start = (h % 4) * 64 + key_row * 8
                bias[s, h // 4, start : start + 8, :] = both


def kernel(
    latent_hbm, w_expand, taps, down_t, up, w_project, gains, w_in_hbm, w_o_hbm, offsets, w_up_hbm, w_down_hbm,
    out,
    latent, w_in, w_o, w_up, w_down, w_vt, bias, gated,
    flat, lat, edge_l, edge_r, halo_l, halo_r, halo_t, halo_b, corners, hid, hid_edge, act,
    total, ar1, ar2, conv, fwd_send, fwd_recv, back_send,
    load_sems, send_sems, recv_sems, ar_send, ar_recv, fs_sems, fr_sems, bs_sems, br_sems,
):
    row, col = lax.axis_index("row"), lax.axis_index("col")
    core, g = lax.rem(row, 2), row // 2
    me = g * 8 + col
    up_row, dn_row = lax.rem(row + ROWS - 1, ROWS), lax.rem(row + 1, ROWS)
    lf, rt = lax.rem(col + COLS - 1, COLS), lax.rem(col + 1, COLS)
    z, ylo, yhi, x = g // 2, lax.rem(g, 2), col // 4, lax.rem(col, 4)
    y = yhi * 2 + ylo

    def partner(o):
        dz = lax.rem(o, 4)
        x2 = lax.rem(x + o // 4 + dz, 4)
        y2 = lax.rem(y + o // 16 + dz, 4)
        z2 = lax.rem(z + dz, 4)
        g2, col2 = z2 * 2 + lax.rem(y2, 2), (y2 // 2) * 4 + x2
        return g2 * 8 + col2, (g2 * 2 + core, col2)

    loads = [
        pltpu.make_async_copy(src, dst, load_sems.at[i])
        for i, (src, dst) in enumerate(
            ((latent_hbm, latent), (w_in_hbm, w_in), (w_o_hbm, w_o), (w_up_hbm, w_up), (w_down_hbm, w_down)))
    ]
    for load in loads:
        load.start()

    barrier = pltpu.get_barrier_semaphore()
    for who in ((row, lf), (row, rt), (up_row, col), (dn_row, col), (up_row, lf), (up_row, rt), (dn_row, lf), (dn_row, rt)):
        pl.semaphore_signal(barrier, inc=1, device_id=who, device_id_type=MESH)

    def greet_row(o, c):
        pl.semaphore_signal(barrier, inc=1, device_id=(lax.rem(row + o, ROWS), col), device_id_type=MESH)
        return c

    def greet_col(o, c):
        pl.semaphore_signal(barrier, inc=1, device_id=(row, lax.rem(col + o, COLS)), device_id_type=MESH)
        return c

    def greet_partner(o, c):
        t = lax.rem(me + o, 64)
        pl.semaphore_signal(barrier, inc=1, device_id=((t // 8) * 2 + core, lax.rem(t, 8)), device_id_type=MESH)
        return c

    lax.fori_loop(1, ROWS, greet_row, 0)
    lax.fori_loop(1, COLS, greet_col, 0)
    lax.fori_loop(1, 64, greet_partner, 0)
    loads[0].wait()

    def spread(y, c):
        put(flat, pl.ds(pl.multiple_of(y * 128, 128), 128), latent[y].astype(F32))
        for v in range(8):
            for j in range(2):
                lat[j, y, v] = flat[j, pl.ds(y * 128 + v, 16, stride=8), :].astype(BF)
        return c

    lax.fori_loop(0, 32, spread, 0)
    edge_l[...] = take(flat, 0, 32, 128).astype(BF)
    edge_r[...] = take(flat, 127, 32, 128).astype(BF)
    pl.semaphore_wait(barrier, 8 + ROWS - 1 + COLS - 1 + 63)
    first, last = pl.ds(0, 16), pl.ds(16, 16)
    moves = (
        (edge_l, halo_r, (row, lf)),
        (edge_r, halo_l, (row, rt)),
        (lat.at[:, 0], halo_b, (up_row, col)),
        (lat.at[:, 31], halo_t, (dn_row, col)),
        (edge_l.at[first], corners.at[3], (up_row, lf)),
        (edge_r.at[first], corners.at[2], (up_row, rt)),
        (edge_l.at[last], corners.at[1], (dn_row, lf)),
        (edge_r.at[last], corners.at[0], (dn_row, rt)),
    )
    copies = []
    for i, (src, dst, who) in enumerate(moves):
        copy = pltpu.make_async_remote_copy(
            src_ref=src, dst_ref=dst, send_sem=send_sems.at[i], recv_sem=recv_sems.at[i], device_id=who, device_id_type=MESH
        )
        copy.start()
        copies.append(copy)

    def expand(i, c):
        rows = pl.ds(i * EXPAND_ROWS, EXPAND_ROWS)
        n = EXPAND_ROWS * 128
        cells = jnp.concatenate([lat[0, rows].reshape(n, 128), lat[1, rows].reshape(n, 128)], axis=1)
        for t in range(4):
            h = twice_gelu(dot(cells, w_expand[:, t * 256 : t * 256 + 256]).astype(BF))
            for j in range(2):
                hid[2 * t + j, pl.ds(1 + i * EXPAND_ROWS, EXPAND_ROWS), 1:9] = lanes(h, j).reshape(EXPAND_ROWS, 8, 16, 128)
        return c

    lax.fori_loop(0, 32 // EXPAND_ROWS, expand, 0)
    for copy in copies:
        copy.wait()
    zero = jnp.zeros((), BF)
    top = jnp.concatenate([halo_t[0].reshape(128, 128), halo_t[1].reshape(128, 128)], axis=1)
    bottom = jnp.concatenate([halo_b[0].reshape(128, 128), halo_b[1].reshape(128, 128)], axis=1)
    top = jnp.where(row > 0, top, zero)
    bottom = jnp.where(row < ROWS - 1, bottom, zero)
    left = jnp.concatenate([
        halo_l[...], jnp.where(row > 0, corners[0], zero), jnp.where(row < ROWS - 1, corners[2], zero)], axis=0)
    right = jnp.concatenate([
        halo_r[...], jnp.where(row > 0, corners[1], zero), jnp.where(row < ROWS - 1, corners[3], zero)], axis=0)
    left = jnp.where(col > 0, left, zero)
    right = jnp.where(col < COLS - 1, right, zero)
    around = jnp.concatenate([top, bottom, left, right], axis=0)
    for t in range(4):
        h = twice_gelu(dot(around, w_expand[:, t * 256 : t * 256 + 256]).astype(BF))
        for j in range(2):
            part = lanes(h, j)
            hid[2 * t + j, 0, 1:9] = part[:128].reshape(8, 16, 128)
            hid[2 * t + j, 33, 1:9] = part[128:256].reshape(8, 16, 128)
            hid_edge[2 * t + j] = part[256:].astype(F32)

    place_n = lax.broadcasted_iota(jnp.int32, (16, 128), 0)

    def wrap(y, c):
        place = jnp.where(y == 0, 47, jnp.where(y == 33, 48, y - 1))
        for t in range(8):
            before = pltpu.roll(hid[t, y, 8].astype(F32), 1, 0)
            hid[t, y, 0] = jnp.where(place_n == 0, hid_edge[t, pl.ds(place, 1), :], before).astype(BF)
            after = pltpu.roll(hid[t, y, 1].astype(F32), 15, 0)
            hid[t, y, 9] = jnp.where(place_n == 15, hid_edge[t, pl.ds(place + 64, 1), :], after).astype(BF)
        return c

    lax.fori_loop(0, 34, wrap, 0)

    for t in range(8):
        weights = [
            jnp.broadcast_to(taps[i // 3, i % 3 : i % 3 + 1, t * 128 : t * 128 + 128].astype(F32) * 0.5, (16, 128)).astype(BF)
            for i in range(9)
        ]

        def depthwise(y, sums):
            acc = None
            for r in range(3):
                cells = hid[t, y + r]
                for s in range(3):
                    term = weights[r * 3 + s][None] * cells[s : s + 8]
                    acc = term if acc is None else acc + term
            a = twice_gelu(acc)
            act[t, y] = a
            b = a[:4] + a[4:]
            b = b[:2] + b[2:]
            return sums + (b[0] + b[1]).astype(F32)

        sums = lax.fori_loop(0, 32, depthwise, jnp.zeros((16, 128), F32))
        total[t : t + 1, :] = jnp.sum(sums, axis=0, keepdims=True)

    ar1[row] = total[...]

    def send_row(o, c):
        pltpu.make_async_remote_copy(
            src_ref=total, dst_ref=ar1.at[row], send_sem=ar_send.at[0], recv_sem=ar_recv.at[0],
            device_id=(lax.rem(row + o, ROWS), col), device_id_type=MESH).start()
        return c

    lax.fori_loop(1, ROWS, send_row, 0)
    for load in loads[1:]:
        load.wait()
    for s in range(2):
        w_vt[s] = w_in[s, :, 512:].astype(F32).T.astype(BF)
    bias_tables(offsets, flat, bias)
    rest = ar1.at[pl.ds(0, ROWS - 1)]
    pltpu.make_async_copy(rest, rest, ar_recv.at[0]).wait()
    pltpu.make_async_copy(rest, rest, ar_send.at[0]).wait()
    ar2[col] = jnp.sum(ar1[...], axis=0)

    def send_col(o, c):
        pltpu.make_async_remote_copy(
            src_ref=ar2.at[col], dst_ref=ar2.at[col], send_sem=ar_send.at[1], recv_sem=ar_recv.at[1],
            device_id=(row, lax.rem(col + o, COLS)), device_id_type=MESH).start()
        return c

    lax.fori_loop(1, COLS, send_col, 0)
    rest = ar2.at[pl.ds(0, COLS - 1)]
    pltpu.make_async_copy(rest, rest, ar_recv.at[1]).wait()
    pltpu.make_async_copy(rest, rest, ar_send.at[1]).wait()
    total[...] = jnp.sum(ar2[...], axis=0) * (0.5 / (512 * 1024))
    squeeze = jnp.concatenate([total[i : i + 1, :] for i in range(8)], axis=1)
    squeeze = jnp.broadcast_to(squeeze, (8, 1024))
    gate = lax.dot_general(
        squeeze, down_t[...].astype(F32), NT, precision=lax.Precision.HIGHEST, preferred_element_type=F32)
    gate = gate * jax.nn.sigmoid(gate)
    excite = jax.nn.sigmoid(
        jnp.dot(gate, up[...].astype(F32), precision=lax.Precision.HIGHEST, preferred_element_type=F32))
    excite = excite.T[:, 0:1] * 0.5
    gated[...] = (w_project[...].astype(F32) * excite).astype(BF)

    weights = (gains, w_in, w_vt, w_o, w_up, w_down, bias)

    def forward(k, c):
        cells = jnp.concatenate([act[t, pl.ds(k * 8, 8)].reshape(1024, 128) for t in range(8)], axis=1)
        put(conv, pl.ds(0, 1024), dot(cells, gated[...]))
        windows = []
        for m in range(8):
            short = latent[pl.ds(k * 8, 8), m * 16 : m * 16 + 16, :].astype(F32)
            for j in range(2):
                branch = take(conv, 2 * m + j, 64, 16)
                windows.append((branch + short[:, j * 8 : j * 8 + 8].reshape(64, 256)).astype(BF).astype(F32))
        done = section_rows(jnp.concatenate(windows, axis=0), 0, *weights)
        for u in range(8):
            line = jnp.concatenate([done[n * 64 + u * 8 : n * 64 + u * 8 + 8] for n in range(16)], axis=0)
            fwd_send[k, u * 8 : u * 8 + 8] = line.astype(BF).reshape(8, 16, 256)
        pltpu.make_async_copy(fwd_send.at[k, me], fwd_recv.at[k, me], fr_sems.at[k]).start()

        def send(o, c2):
            t, who = partner(o)
            pltpu.make_async_remote_copy(
                src_ref=fwd_send.at[k, t], dst_ref=fwd_recv.at[k, me], send_sem=fs_sems.at[k], recv_sem=fr_sems.at[k],
                device_id=who, device_id_type=MESH).start()
            return c2

        lax.fori_loop(1, 64, send, 0)
        return c

    lax.fori_loop(0, BANDS, forward, 0)

    def backward(k, c):
        pltpu.make_async_copy(fwd_recv.at[k], fwd_recv.at[k], fr_sems.at[k]).wait()
        put(conv, pl.ds(0, 1024), fwd_recv[k].reshape(1024, 256).astype(F32))
        windows = jnp.concatenate([take(conv, n, 64, 16) for n in range(16)], axis=0)
        put(conv, pl.ds(0, 1024), section_rows(windows, 1, *weights))
        for t in range(64):
            back_send[k, t] = take(conv, t, 16, 64).astype(BF)
        here = out.at[k * 8 + g, pl.ds(pl.multiple_of(col * 16, 16), 16)]
        pltpu.make_async_copy(back_send.at[k, me], here, br_sems.at[k]).start()

        def send(o, c2):
            t, who = partner(o)
            pltpu.make_async_remote_copy(
                src_ref=back_send.at[k, t], dst_ref=here, send_sem=bs_sems.at[k], recv_sem=br_sems.at[k],
                device_id=who, device_id_type=MESH).start()
            return c2

        lax.fori_loop(1, 64, send, 0)
        return c

    lax.fori_loop(0, BANDS, backward, 0)

    def finish(k, c):
        band = out.at[pl.ds(k * 8, 8)]
        pltpu.make_async_copy(band, band, br_sems.at[k]).wait()
        for sems, buf in ((fs_sems, fwd_send), (bs_sems, back_send)):
            sent = buf.at[k, pl.ds(0, 63)]
            pltpu.make_async_copy(sent, sent, sems.at[k]).wait()
        return c

    lax.fori_loop(0, BANDS, finish, 0)


EXPAND_ROWS = 8


def per_device(
    latent, w_expand, w_depth, squeeze_down, squeeze_up, w_project,
    norm_gain, attend_in, attend_out, offset_bias, mixer_up, mixer_down,
):
    vmem = pl.BlockSpec(memory_space=pltpu.VMEM)
    hbm = pl.BlockSpec(memory_space=pl.ANY)
    block = (BANDS, 64, 16, 256)
    dma = pltpu.SemaphoreType.DMA
    return pl.pallas_call(
        kernel,
        out_shape=jax.ShapeDtypeStruct((32, 128, 256), BF),
        in_specs=[hbm, vmem, vmem, vmem, vmem, vmem, vmem, hbm, hbm, vmem, hbm, hbm],
        out_specs=hbm,
        scratch_shapes=[
            pltpu.VMEM((32, 128, 256), BF),
            pltpu.VMEM((2, 256, 768), BF),
            pltpu.VMEM((2, 256, 256), BF),
            pltpu.VMEM((2, 256, 1024), BF),
            pltpu.VMEM((2, 1024, 256), BF),
            pltpu.VMEM((2, 256, 256), BF),
            pltpu.VMEM((2, 2, 256, 128), F32),
            pltpu.VMEM((1024, 256), BF),
            pltpu.VMEM((2, 4096, 128), F32),
            pltpu.VMEM((2, 32, 8, 16, 128), BF),
            pltpu.VMEM((32, 256), BF),
            pltpu.VMEM((32, 256), BF),
            pltpu.VMEM((32, 256), BF),
            pltpu.VMEM((32, 256), BF),
            pltpu.VMEM((2, 8, 16, 128), BF),
            pltpu.VMEM((2, 8, 16, 128), BF),
            pltpu.VMEM((4, 16, 256), BF),
            pltpu.VMEM((8, 34, 10, 16, 128), BF),
            pltpu.VMEM((8, 128, 128), F32),
            pltpu.VMEM((8, 32, 8, 16, 128), BF),
            pltpu.VMEM((8, 128), F32),
            pltpu.VMEM((ROWS, 8, 128), F32),
            pltpu.VMEM((COLS, 8, 128), F32),
            pltpu.VMEM((2, 1024, 128), F32),
            pltpu.VMEM(block, BF),
            pltpu.VMEM(block, BF),
            pltpu.VMEM(block, BF),
            dma((5,)),
            dma((8,)),
            dma((8,)),
            dma((2,)),
            dma((2,)),
            dma((BANDS,)),
            dma((BANDS,)),
            dma((BANDS,)),
            dma((BANDS,)),
        ],
        compiler_params=pltpu.CompilerParams(collective_id=0, has_side_effects=True, vmem_limit_bytes=60 << 20),
        name="block",
    )(
        latent, w_expand, w_depth, squeeze_down.T, squeeze_up, w_project,
        norm_gain, attend_in, attend_out, offset_bias.transpose(0, 2, 1, 3), mixer_up, mixer_down,
    )


def solution(mesh):
    in_specs = (P("row", "col", None),) + (P(),) * 11
    return jax.shard_map(
        per_device, mesh=mesh, in_specs=in_specs, out_specs=P("row", "col", None), check_vma=False
    )
```

time: 169 us -> 108 us (0.64)
  Pallas kernels: 155 us -> 105 us
  local copies, waits for them, and re-layouts: 7.78 us -> 3.13 us
  other arithmetic: 4.06 us -> 0 us
    pallas_call x2 -> x1, Pallas kernels: 155 us -> 105 us  [per_device(): pl.pallas_call(kernel, out_shape=jax.ShapeDtypeStruct((32, 128, 256), BF)...]
    transpose x1 -> x0, local copies, waits for them, and re-layouts: 3.17 us -> none  [per_device(): tiles = returned.reshape(BANDS, 16, WIN, WIN, 256).transpose(0, 2, 1, 3, 4)]
    mul x3 -> x0, other arithmetic: 2.94 us -> none  [the longest x1 1.06 us: per_device(): mixer_down * 0.5]
where the time goes in v2:
time: 108 us
  Pallas kernels  105 us (97%)
  local copies, waits for them, and re-layouts  3.13 us (3%)
    pallas_call x1, Pallas kernels, per_device(): pl.pallas_call(kernel, out_shape=jax.ShapeDtypeStruct((32, 128, 256), BF)...  105 us
    unnamed x1, local copies, waits for them, and re-layouts  3.13 us

profile of v2, /device:TPU:1, one launch (start us, length us, event | category | flops | bytes accessed | tf_op | source)
XLA Modules:
  0.0 108.1 jit_solution(616489883580812336)
XLA Ops:
  0.0 105.0 %block.1 = bf16[32,128,256]{2,1,0:T(8,128)(2,1)} custom-call(bf16[32,128,256]{2,1,0:T(8,128)(2,1)} %latent_hbm.1, bf16[256,1024]{1,0:T(8,128)(2,1)} %w_expand.1, bf16[3,3,1024]{2,1,0:T(4,128)(2,1)} %taps.1, bf16[64,1024]{1,0:T(8,128)(2,1)} %bitcast.2, bf16[64,1024]{1,0:T(8,128)(2,1)} %up.1, bf16[1024,256]{1,0:T(8,128)(2,1)} %w_project.1, ...), custom_call_target="tpu_custom_call" | custom-call | tf_op jit(solution)/shard_map/block/pallas_call | solution.py:407
  105.0 3.1 %copy.14 = bf16[32,128,256]{2,1,0:T(8,128)(2,1)} copy(bf16[32,128,256]{2,1,0:T(8,128)(2,1)} %block.1) | data formatting | bytes 4194304

commit v3 on v2

--- a/solution.py
+++ b/solution.py
@@ -97,11 +97,18 @@
         r = slice(p * 128, p * 128 + 128)
         mixed = attention_pair(qk[r, :256], qk[r, 256:], vt[:, r], bias, s)
         mixes.append(mixed.T.astype(BF))
-    mix = jnp.concatenate(mixes, axis=0)
-    attended = (x + dot(mix, w_o[s])).astype(BF).astype(F32)
-    normed = normalise(attended, gains[s, 1:2])
-    up = [twice_gelu(dot(normed, w_up[s, :, t * 256 : t * 256 + 256]).astype(BF)) for t in range(4)]
-    return attended + 0.5 * dot(jnp.concatenate(up, axis=1), w_down[s])
+    closed = []
+    for i in range(0, n // 128, 4):
+        mix = jnp.concatenate(mixes[i : i + 4], axis=0)
+        closed.append((x[i * 128 : i * 128 + 512] + dot(mix, w_o[s])).astype(BF).astype(F32))
+    normed = jnp.concatenate([normalise(a, gains[s, 1:2]) for a in closed], axis=0)
+    attended = jnp.concatenate(closed, axis=0)
+    low = []
+    for r in range(n // 256):
+        rows = normed[r * 256 : r * 256 + 256]
+        up = [twice_gelu(dot(rows, w_up[s, :, t * 256 : t * 256 + 256]).astype(BF)) for t in range(4)]
+        low.append(dot(jnp.concatenate(up, axis=1), w_down[s]))
+    return attended + 0.5 * jnp.concatenate(low, axis=0)
 
 
 def bias_tables(offsets, flat, bias):
@@ -155,13 +162,24 @@
     z, ylo, yhi, x = g // 2, lax.rem(g, 2), col // 4, lax.rem(col, 4)
     y = yhi * 2 + ylo
 
-    def partner(o):
-        dz = lax.rem(o, 4)
-        x2 = lax.rem(x + o // 4 + dz, 4)
-        y2 = lax.rem(y + o // 16 + dz, 4)
-        z2 = lax.rem(z + dz, 4)
-        g2, col2 = z2 * 2 + lax.rem(y2, 2), (y2 // 2) * 4 + x2
-        return g2 * 8 + col2, (g2 * 2 + core, col2)
+    xs = [lax.rem(x + d, 4) for d in range(4)]
+    ys = [lax.rem(y + d, 4) for d in range(4)]
+    zs = [lax.rem(z + d, 4) for d in range(4)]
+    groups = [[zs[dz] * 2 + lax.rem(ys[dy], 2) for dy in range(4)] for dz in range(4)]
+    columns = [[(ys[dy] // 2) * 4 + xs[dx] for dx in range(4)] for dy in range(4)]
+
+    parity = lax.rem(x + y + z, 2)
+    depths = [zs[dz] * 16 for dz in range(4)]
+    heights = [(ys[dy] // 2) * 8 + lax.rem(ys[dy], 2) * 2 for dy in range(4)]
+    halves = [xs[dx] // 2 for dx in range(4)]
+    own = z * 16 + (y // 2) * 8 + parity * 4 + lax.rem(y, 2) * 2 + x // 2
+
+    def exchange(source, target, send_sem, recv_sem, offsets):
+        for dx, dy, dz in offsets:
+            group, column = groups[dz][dy], columns[dy][dx]
+            pltpu.make_async_remote_copy(
+                src_ref=source(group * 8 + column, depths[dz] + heights[dy] + halves[dx]), dst_ref=target,
+                send_sem=send_sem, recv_sem=recv_sem, device_id=(group * 2 + core, column), device_id_type=MESH).start()
 
     loads = [
         pltpu.make_async_copy(src, dst, load_sems.at[i])
@@ -175,41 +193,19 @@
     for who in ((row, lf), (row, rt), (up_row, col), (dn_row, col), (up_row, lf), (up_row, rt), (dn_row, lf), (dn_row, rt)):
         pl.semaphore_signal(barrier, inc=1, device_id=who, device_id_type=MESH)
 
-    def greet_row(o, c):
-        pl.semaphore_signal(barrier, inc=1, device_id=(lax.rem(row + o, ROWS), col), device_id_type=MESH)
-        return c
-
-    def greet_col(o, c):
-        pl.semaphore_signal(barrier, inc=1, device_id=(row, lax.rem(col + o, COLS)), device_id_type=MESH)
-        return c
-
-    def greet_partner(o, c):
-        t = lax.rem(me + o, 64)
-        pl.semaphore_signal(barrier, inc=1, device_id=((t // 8) * 2 + core, lax.rem(t, 8)), device_id_type=MESH)
-        return c
-
-    lax.fori_loop(1, ROWS, greet_row, 0)
-    lax.fori_loop(1, COLS, greet_col, 0)
-    lax.fori_loop(1, 64, greet_partner, 0)
+    for dx, dy, dz in ORDER:
+        pl.semaphore_signal(barrier, inc=1, device_id=(groups[dz][dy] * 2 + core, columns[dy][dx]), device_id_type=MESH)
     loads[0].wait()
 
-    def spread(y, c):
-        put(flat, pl.ds(pl.multiple_of(y * 128, 128), 128), latent[y].astype(F32))
-        for v in range(8):
-            for j in range(2):
-                lat[j, y, v] = flat[j, pl.ds(y * 128 + v, 16, stride=8), :].astype(BF)
-        return c
-
-    lax.fori_loop(0, 32, spread, 0)
-    edge_l[...] = take(flat, 0, 32, 128).astype(BF)
-    edge_r[...] = take(flat, 127, 32, 128).astype(BF)
-    pl.semaphore_wait(barrier, 8 + ROWS - 1 + COLS - 1 + 63)
+    edge_l[...] = latent[:, :16, :].astype(F32)[:, 0, :].astype(BF)
+    edge_r[...] = latent[:, 112:, :].astype(F32)[:, 15, :].astype(BF)
+    pl.semaphore_wait(barrier, 8 + 63)
     first, last = pl.ds(0, 16), pl.ds(16, 16)
     moves = (
         (edge_l, halo_r, (row, lf)),
         (edge_r, halo_l, (row, rt)),
-        (lat.at[:, 0], halo_b, (up_row, col)),
-        (lat.at[:, 31], halo_t, (dn_row, col)),
+        (latent.at[0], halo_b, (up_row, col)),
+        (latent.at[31], halo_t, (dn_row, col)),
         (edge_l.at[first], corners.at[3], (up_row, lf)),
         (edge_r.at[first], corners.at[2], (up_row, rt)),
         (edge_l.at[last], corners.at[1], (dn_row, lf)),
@@ -223,6 +219,14 @@
         copy.start()
         copies.append(copy)
 
+    def spread(y, c):
+        put(flat, pl.ds(pl.multiple_of(y * 128, 128), 128), latent[y].astype(F32))
+        for v in range(8):
+            for j in range(2):
+                lat[j, y, v] = flat[j, pl.ds(y * 128 + v, 16, stride=8), :].astype(BF)
+        return c
+
+    lax.fori_loop(0, 32, spread, 0)
     def expand(i, c):
         rows = pl.ds(i * EXPAND_ROWS, EXPAND_ROWS)
         n = EXPAND_ROWS * 128
@@ -237,17 +241,18 @@
     for copy in copies:
         copy.wait()
     zero = jnp.zeros((), BF)
-    top = jnp.concatenate([halo_t[0].reshape(128, 128), halo_t[1].reshape(128, 128)], axis=1)
-    bottom = jnp.concatenate([halo_b[0].reshape(128, 128), halo_b[1].reshape(128, 128)], axis=1)
-    top = jnp.where(row > 0, top, zero)
-    bottom = jnp.where(row < ROWS - 1, bottom, zero)
+    edge_rows = []
+    for i, (halo, inside) in enumerate(((halo_t, row > 0), (halo_b, row < ROWS - 1))):
+        put(flat, pl.ds(i * 128, 128), halo[...].astype(F32))
+        cells = jnp.concatenate([take(flat, i * 128 + v, 16, 8) for v in range(8)], axis=0)
+        edge_rows.append(jnp.where(inside, cells, 0.0).astype(BF))
     left = jnp.concatenate([
         halo_l[...], jnp.where(row > 0, corners[0], zero), jnp.where(row < ROWS - 1, corners[2], zero)], axis=0)
     right = jnp.concatenate([
         halo_r[...], jnp.where(row > 0, corners[1], zero), jnp.where(row < ROWS - 1, corners[3], zero)], axis=0)
     left = jnp.where(col > 0, left, zero)
     right = jnp.where(col < COLS - 1, right, zero)
-    around = jnp.concatenate([top, bottom, left, right], axis=0)
+    around = jnp.concatenate(edge_rows + [left, right], axis=0)
     for t in range(4):
         h = twice_gelu(dot(around, w_expand[:, t * 256 : t * 256 + 256]).astype(BF))
         for j in range(2):
@@ -258,16 +263,17 @@
 
     place_n = lax.broadcasted_iota(jnp.int32, (16, 128), 0)
 
-    def wrap(y, c):
-        place = jnp.where(y == 0, 47, jnp.where(y == 33, 48, y - 1))
-        for t in range(8):
-            before = pltpu.roll(hid[t, y, 8].astype(F32), 1, 0)
-            hid[t, y, 0] = jnp.where(place_n == 0, hid_edge[t, pl.ds(place, 1), :], before).astype(BF)
-            after = pltpu.roll(hid[t, y, 1].astype(F32), 15, 0)
-            hid[t, y, 9] = jnp.where(place_n == 15, hid_edge[t, pl.ds(place + 64, 1), :], after).astype(BF)
-        return c
-
-    lax.fori_loop(0, 34, wrap, 0)
+    def wrap(i, c):
+        for y in (2 * i, 2 * i + 1):
+            place = jnp.where(y == 0, 47, jnp.where(y == 33, 48, y - 1))
+            for t in range(8):
+                before = pltpu.roll(hid[t, y, 8].astype(F32), 1, 0)
+                hid[t, y, 0] = jnp.where(place_n == 0, hid_edge[t, pl.ds(place, 1), :], before).astype(BF)
+                after = pltpu.roll(hid[t, y, 1].astype(F32), 15, 0)
+                hid[t, y, 9] = jnp.where(place_n == 15, hid_edge[t, pl.ds(place + 64, 1), :], after).astype(BF)
+        return c
+
+    lax.fori_loop(0, 17, wrap, 0)
 
     for t in range(8):
         weights = [
@@ -275,53 +281,43 @@
             for i in range(9)
         ]
 
-        def depthwise(y, sums):
-            acc = None
-            for r in range(3):
+        def depthwise(i, sums):
+            y = i * DEPTH_ROWS
+            accs = [None] * DEPTH_ROWS
+            for r in range(DEPTH_ROWS + 2):
                 cells = hid[t, y + r]
-                for s in range(3):
-                    term = weights[r * 3 + s][None] * cells[s : s + 8]
-                    acc = term if acc is None else acc + term
-            a = twice_gelu(acc)
-            act[t, y] = a
-            b = a[:4] + a[4:]
-            b = b[:2] + b[2:]
-            return sums + (b[0] + b[1]).astype(F32)
-
-        sums = lax.fori_loop(0, 32, depthwise, jnp.zeros((16, 128), F32))
+                for q in range(max(0, r - 2), min(DEPTH_ROWS, r + 1)):
+                    for s in range(3):
+                        term = weights[(r - q) * 3 + s][None] * cells[s : s + 8]
+                        accs[q] = term if accs[q] is None else accs[q] + term
+                if r >= 2:
+                    a = twice_gelu(accs[r - 2])
+                    act[t, y + r - 2] = a
+                    b = a[:4] + a[4:]
+                    b = b[:2] + b[2:]
+                    sums = sums + (b[0] + b[1]).astype(F32)
+            return sums
+
+        sums = lax.fori_loop(0, 32 // DEPTH_ROWS, depthwise, jnp.zeros((16, 128), F32))
         total[t : t + 1, :] = jnp.sum(sums, axis=0, keepdims=True)
 
-    ar1[row] = total[...]
-
-    def send_row(o, c):
-        pltpu.make_async_remote_copy(
-            src_ref=total, dst_ref=ar1.at[row], send_sem=ar_send.at[0], recv_sem=ar_recv.at[0],
-            device_id=(lax.rem(row + o, ROWS), col), device_id_type=MESH).start()
-        return c
-
-    lax.fori_loop(1, ROWS, send_row, 0)
+    ar1[me] = total[...]
+    exchange(lambda device, share: total, ar1.at[me], ar_send.at[0], ar_recv.at[0], ORDER)
     for load in loads[1:]:
         load.wait()
     for s in range(2):
         w_vt[s] = w_in[s, :, 512:].astype(F32).T.astype(BF)
     bias_tables(offsets, flat, bias)
-    rest = ar1.at[pl.ds(0, ROWS - 1)]
+    rest = ar1.at[pl.ds(0, 63)]
     pltpu.make_async_copy(rest, rest, ar_recv.at[0]).wait()
-    pltpu.make_async_copy(rest, rest, ar_send.at[0]).wait()
-    ar2[col] = jnp.sum(ar1[...], axis=0)
-
-    def send_col(o, c):
-        pltpu.make_async_remote_copy(
-            src_ref=ar2.at[col], dst_ref=ar2.at[col], send_sem=ar_send.at[1], recv_sem=ar_recv.at[1],
-            device_id=(row, lax.rem(col + o, COLS)), device_id_type=MESH).start()
-        return c
-
-    lax.fori_loop(1, COLS, send_col, 0)
-    rest = ar2.at[pl.ds(0, COLS - 1)]
-    pltpu.make_async_copy(rest, rest, ar_recv.at[1]).wait()
-    pltpu.make_async_copy(rest, rest, ar_send.at[1]).wait()
-    total[...] = jnp.sum(ar2[...], axis=0) * (0.5 / (512 * 1024))
-    squeeze = jnp.concatenate([total[i : i + 1, :] for i in range(8)], axis=1)
+    ar2[core] = jnp.sum(ar1[...], axis=0)
+    sibling = pltpu.make_async_remote_copy(
+        src_ref=ar2.at[core], dst_ref=ar2.at[core], send_sem=ar_send.at[1], recv_sem=ar_recv.at[1],
+        device_id=(g * 2 + 1 - core, col), device_id_type=MESH)
+    sibling.start()
+    sibling.wait()
+    mean = jnp.sum(ar2[...], axis=0) * (0.5 / (512 * 1024))
+    squeeze = jnp.concatenate([mean[i : i + 1, :] for i in range(8)], axis=1)
     squeeze = jnp.broadcast_to(squeeze, (8, 1024))
     gate = lax.dot_general(
         squeeze, down_t[...].astype(F32), NT, precision=lax.Precision.HIGHEST, preferred_element_type=F32)
@@ -348,14 +344,7 @@
             fwd_send[k, u * 8 : u * 8 + 8] = line.astype(BF).reshape(8, 16, 256)
         pltpu.make_async_copy(fwd_send.at[k, me], fwd_recv.at[k, me], fr_sems.at[k]).start()
 
-        def send(o, c2):
-            t, who = partner(o)
-            pltpu.make_async_remote_copy(
-                src_ref=fwd_send.at[k, t], dst_ref=fwd_recv.at[k, me], send_sem=fs_sems.at[k], recv_sem=fr_sems.at[k],
-                device_id=who, device_id_type=MESH).start()
-            return c2
-
-        lax.fori_loop(1, 64, send, 0)
+        exchange(lambda device, share: fwd_send.at[k, device], fwd_recv.at[k, me], fs_sems.at[k], fr_sems.at[k], ORDER)
         return c
 
     lax.fori_loop(0, BANDS, forward, 0)
@@ -367,23 +356,16 @@
         put(conv, pl.ds(0, 1024), section_rows(windows, 1, *weights))
         for t in range(64):
             back_send[k, t] = take(conv, t, 16, 64).astype(BF)
-        here = out.at[k * 8 + g, pl.ds(pl.multiple_of(col * 16, 16), 16)]
+        here = out.at[k * 16 + g * 2 + col // 4, pl.ds(pl.multiple_of(lax.rem(col, 4) * 16, 16), 16)]
         pltpu.make_async_copy(back_send.at[k, me], here, br_sems.at[k]).start()
 
-        def send(o, c2):
-            t, who = partner(o)
-            pltpu.make_async_remote_copy(
-                src_ref=back_send.at[k, t], dst_ref=here, send_sem=bs_sems.at[k], recv_sem=br_sems.at[k],
-                device_id=who, device_id_type=MESH).start()
-            return c2
-
-        lax.fori_loop(1, 64, send, 0)
+        exchange(lambda device, share: back_send.at[k, device], here, bs_sems.at[k], br_sems.at[k], ORDER)
         return c
 
     lax.fori_loop(0, BANDS, backward, 0)
 
     def finish(k, c):
-        band = out.at[pl.ds(k * 8, 8)]
+        band = out.at[pl.ds(k * 16, 16)]
         pltpu.make_async_copy(band, band, br_sems.at[k]).wait()
         for sems, buf in ((fs_sems, fwd_send), (bs_sems, back_send)):
             sent = buf.at[k, pl.ds(0, 63)]
@@ -391,9 +373,21 @@
         return c
 
     lax.fori_loop(0, BANDS, finish, 0)
+    pltpu.make_async_copy(rest, rest, ar_send.at[0]).wait()
 
 
 EXPAND_ROWS = 8
+DEPTH_ROWS = 4
+
+
+def hops(offset):
+    return sum(min(d, 4 - d) for d in offset)
+
+
+ORDER = sorted(
+    ((dx, dy, dz) for dx in range(4) for dy in range(4) for dz in range(4) if (dx, dy, dz) != (0, 0, 0)),
+    key=lambda o: (-hops(o), min(o, tuple(-d % 4 for d in o))[::-1]),
+)
 
 
 def per_device(
@@ -406,7 +400,7 @@
     dma = pltpu.SemaphoreType.DMA
     return pl.pallas_call(
         kernel,
-        out_shape=jax.ShapeDtypeStruct((32, 128, 256), BF),
+        out_shape=jax.ShapeDtypeStruct((64, 64, 256), BF),
         in_specs=[hbm, vmem, vmem, vmem, vmem, vmem, vmem, hbm, hbm, vmem, hbm, hbm],
         out_specs=hbm,
         scratch_shapes=[
@@ -424,15 +418,15 @@
             pltpu.VMEM((32, 256), BF),
             pltpu.VMEM((32, 256), BF),
             pltpu.VMEM((32, 256), BF),
-            pltpu.VMEM((2, 8, 16, 128), BF),
-            pltpu.VMEM((2, 8, 16, 128), BF),
+            pltpu.VMEM((128, 256), BF),
+            pltpu.VMEM((128, 256), BF),
             pltpu.VMEM((4, 16, 256), BF),
             pltpu.VMEM((8, 34, 10, 16, 128), BF),
             pltpu.VMEM((8, 128, 128), F32),
             pltpu.VMEM((8, 32, 8, 16, 128), BF),
             pltpu.VMEM((8, 128), F32),
-            pltpu.VMEM((ROWS, 8, 128), F32),
-            pltpu.VMEM((COLS, 8, 128), F32),
+            pltpu.VMEM((64, 8, 128), F32),
+            pltpu.VMEM((2, 8, 128), F32),
             pltpu.VMEM((2, 1024, 128), F32),
             pltpu.VMEM(block, BF),
             pltpu.VMEM(block, BF),
@@ -447,12 +441,12 @@
             dma((BANDS,)),
             dma((BANDS,)),
         ],
-        compiler_params=pltpu.CompilerParams(collective_id=0, has_side_effects=True, vmem_limit_bytes=60 << 20),
+        compiler_params=pltpu.CompilerParams(collective_id=0, has_side_effects=True, vmem_limit_bytes=46 << 20),
         name="block",
-    )(
+    )(*(pltpu.with_memory_space_constraint(a, pltpu.HBM) for a in (
         latent, w_expand, w_depth, squeeze_down.T, squeeze_up, w_project,
         norm_gain, attend_in, attend_out, offset_bias.transpose(0, 2, 1, 3), mixer_up, mixer_down,
-    )
+    ))).reshape(32, 128, 256)
 
 
 def solution(mesh):

time: 108 us -> 90.8 us (0.84)
  Pallas kernels: 105 us -> 89.3 us
  local copies, waits for them, and re-layouts: 3.13 us -> 1.32 us
    pallas_call x1, Pallas kernels: 105 us -> 89.3 us  [per_device(): pl.pallas_call(kernel, out_shape=jax.ShapeDtypeStruct((64, 64, 256), BF),...]
    unnamed x1, local copies, waits for them, and re-layouts: 3.13 us -> 1.32 us
where the time goes in v3:
time: 90.8 us; the launch traced here: 90.6 us
  Pallas kernels  89.3 us (98%)
  local copies, waits for them, and re-layouts  1.32 us (1%)
    pallas_call x1, Pallas kernels, per_device(): pl.pallas_call(kernel, out_shape=jax.ShapeDtypeStruct((64, 64, 256), BF),...  89.3 us

profile of v3, /device:TPU:1, one launch (start us, length us, event | category | flops | bytes accessed | tf_op | source)
XLA Modules:
  0.0 90.6 jit_solution(14577698150029591369)
XLA Ops:
  0.0 89.3 %block.1 = bf16[64,64,256]{2,1,0:T(8,128)(2,1)S(1)} custom-call(bf16[32,128,256]{2,1,0:T(8,128)(2,1)} %latent_hbm.1, bf16[256,1024]{1,0:T(8,128)(2,1)} %w_expand.1, bf16[3,3,1024]{2,1,0:T(4,128)(2,1)} %taps.1, bf16[64,1024]{1,0:T(8,128)(2,1)} %bitcast.4, bf16[64,1024]{1,0:T(8,128)(2,1)} %up.1, bf16[1024,256]{1,0:T(8,128)(2,1)} %w_project.1, ...), custom_call_target="tpu_custom_call" | custom-call | tf_op jit(solution)/shard_map/block/pallas_call | solution.py:401
  89.3 1.3 %copy.14 = bf16[32,128,256]{2,1,0:T(8,128)(2,1)} copy(bf16[32,128,256]{2,1,0:T(8,128)(2,1)S(1)} %bitcast.3) | data formatting | bytes 4194304

commit v4 on v3

--- a/solution.py
+++ b/solution.py
@@ -147,9 +147,11 @@
 
 
 def kernel(
-    latent_hbm, w_expand, taps, down_t, up, w_project, gains, w_in_hbm, w_o_hbm, offsets, w_up_hbm, w_down_hbm,
+    latent_hbm, w_expand_hbm, taps_hbm, down_hbm, up_hbm, w_project_hbm, gains_hbm, w_in_hbm, w_o_hbm, offsets_hbm,
+    w_up_hbm, w_down_hbm,
     out,
-    latent, w_in, w_o, w_up, w_down, w_vt, bias, gated,
+    side_l, side_r, latent, w_expand, taps, down_t, up, w_project, gains, w_in, w_o, offsets, w_up, w_down,
+    w_vt, bias, gated,
     flat, lat, edge_l, edge_r, halo_l, halo_r, halo_t, halo_b, corners, hid, hid_edge, act,
     total, ar1, ar2, conv, fwd_send, fwd_recv, back_send,
     load_sems, send_sems, recv_sems, ar_send, ar_recv, fs_sems, fr_sems, bs_sems, br_sems,
@@ -181,11 +183,13 @@
                 src_ref=source(group * 8 + column, depths[dz] + heights[dy] + halves[dx]), dst_ref=target,
                 send_sem=send_sem, recv_sem=recv_sem, device_id=(group * 2 + core, column), device_id_type=MESH).start()
 
-    loads = [
-        pltpu.make_async_copy(src, dst, load_sems.at[i])
-        for i, (src, dst) in enumerate(
-            ((latent_hbm, latent), (w_in_hbm, w_in), (w_o_hbm, w_o), (w_up_hbm, w_up), (w_down_hbm, w_down)))
-    ]
+    pairs = (
+        (latent_hbm.at[:, pl.ds(0, 16), :], side_l), (latent_hbm.at[:, pl.ds(112, 16), :], side_r),
+        (latent_hbm, latent), (w_expand_hbm, w_expand), (taps_hbm, taps), (down_hbm, down_t), (up_hbm, up),
+        (w_project_hbm, w_project), (gains_hbm, gains), (w_in_hbm, w_in), (w_o_hbm, w_o), (offsets_hbm, offsets),
+        (w_up_hbm, w_up), (w_down_hbm, w_down),
+    )
+    loads = [pltpu.make_async_copy(src, dst, load_sems.at[i]) for i, (src, dst) in enumerate(pairs)]
     for load in loads:
         load.start()
 
@@ -196,16 +200,17 @@
     for dx, dy, dz in ORDER:
         pl.semaphore_signal(barrier, inc=1, device_id=(groups[dz][dy] * 2 + core, columns[dy][dx]), device_id_type=MESH)
     loads[0].wait()
-
-    edge_l[...] = latent[:, :16, :].astype(F32)[:, 0, :].astype(BF)
-    edge_r[...] = latent[:, 112:, :].astype(F32)[:, 15, :].astype(BF)
+    loads[1].wait()
+
+    edge_l[...] = side_l[...].astype(F32)[:, 0, :].astype(BF)
+    edge_r[...] = side_r[...].astype(F32)[:, 15, :].astype(BF)
     pl.semaphore_wait(barrier, 8 + 63)
     first, last = pl.ds(0, 16), pl.ds(16, 16)
     moves = (
         (edge_l, halo_r, (row, lf)),
         (edge_r, halo_l, (row, rt)),
-        (latent.at[0], halo_b, (up_row, col)),
-        (latent.at[31], halo_t, (dn_row, col)),
+        (latent_hbm.at[0], halo_b, (up_row, col)),
+        (latent_hbm.at[31], halo_t, (dn_row, col)),
         (edge_l.at[first], corners.at[3], (up_row, lf)),
         (edge_r.at[first], corners.at[2], (up_row, rt)),
         (edge_l.at[last], corners.at[1], (dn_row, lf)),
@@ -219,6 +224,8 @@
         copy.start()
         copies.append(copy)
 
+    loads[2].wait()
+
     def spread(y, c):
         put(flat, pl.ds(pl.multiple_of(y * 128, 128), 128), latent[y].astype(F32))
         for v in range(8):
@@ -237,6 +244,7 @@
                 hid[2 * t + j, pl.ds(1 + i * EXPAND_ROWS, EXPAND_ROWS), 1:9] = lanes(h, j).reshape(EXPAND_ROWS, 8, 16, 128)
         return c
 
+    loads[3].wait()
     lax.fori_loop(0, 32 // EXPAND_ROWS, expand, 0)
     for copy in copies:
         copy.wait()
@@ -261,6 +269,7 @@
             hid[2 * t + j, 33, 1:9] = part[128:256].reshape(8, 16, 128)
             hid_edge[2 * t + j] = part[256:].astype(F32)
 
+    loads[4].wait()
     place_n = lax.broadcasted_iota(jnp.int32, (16, 128), 0)
 
     def wrap(i, c):
@@ -303,7 +312,7 @@
 
     ar1[me] = total[...]
     exchange(lambda device, share: total, ar1.at[me], ar_send.at[0], ar_recv.at[0], ORDER)
-    for load in loads[1:]:
+    for load in loads[5:]:
         load.wait()
     for s in range(2):
         w_vt[s] = w_in[s, :, 512:].astype(F32).T.astype(BF)
@@ -331,7 +340,8 @@
 
     def forward(k, c):
         cells = jnp.concatenate([act[t, pl.ds(k * 8, 8)].reshape(1024, 128) for t in range(8)], axis=1)
-        put(conv, pl.ds(0, 1024), dot(cells, gated[...]))
+        for r in range(0, 1024, 256):
+            put(conv, pl.ds(r, 256), dot(cells[r : r + 256], gated[...]))
         windows = []
         for m in range(8):
             short = latent[pl.ds(k * 8, 8), m * 16 : m * 16 + 16, :].astype(F32)
@@ -394,19 +404,27 @@
     latent, w_expand, w_depth, squeeze_down, squeeze_up, w_project,
     norm_gain, attend_in, attend_out, offset_bias, mixer_up, mixer_down,
 ):
-    vmem = pl.BlockSpec(memory_space=pltpu.VMEM)
     hbm = pl.BlockSpec(memory_space=pl.ANY)
     block = (BANDS, 64, 16, 256)
     dma = pltpu.SemaphoreType.DMA
     return pl.pallas_call(
         kernel,
         out_shape=jax.ShapeDtypeStruct((64, 64, 256), BF),
-        in_specs=[hbm, vmem, vmem, vmem, vmem, vmem, vmem, hbm, hbm, vmem, hbm, hbm],
+        in_specs=[hbm] * 12,
         out_specs=hbm,
         scratch_shapes=[
+            pltpu.VMEM((32, 16, 256), BF),
+            pltpu.VMEM((32, 16, 256), BF),
             pltpu.VMEM((32, 128, 256), BF),
+            pltpu.VMEM((256, 1024), BF),
+            pltpu.VMEM((3, 3, 1024), BF),
+            pltpu.VMEM((64, 1024), BF),
+            pltpu.VMEM((64, 1024), BF),
+            pltpu.VMEM((1024, 256), BF),
+            pltpu.VMEM((2, 2, 256), F32),
             pltpu.VMEM((2, 256, 768), BF),
             pltpu.VMEM((2, 256, 256), BF),
+            pltpu.VMEM((2, 15, 8, 15), F32),
             pltpu.VMEM((2, 256, 1024), BF),
             pltpu.VMEM((2, 1024, 256), BF),
             pltpu.VMEM((2, 256, 256), BF),
@@ -431,7 +449,7 @@
             pltpu.VMEM(block, BF),
             pltpu.VMEM(block, BF),
             pltpu.VMEM(block, BF),
-            dma((5,)),
+            dma((14,)),
             dma((8,)),
             dma((8,)),
             dma((2,)),

time: 90.8 us -> 87.9 us (0.968)
  Pallas kernels: 89.3 us -> 86.5 us
    pallas_call x1, Pallas kernels: 89.3 us -> 86.5 us  [per_device(): pl.pallas_call(kernel, out_shape=jax.ShapeDtypeStruct((64, 64, 256), BF),...]
where the time goes in v4:
time: 87.9 us; the launch traced here: 87.8 us
  Pallas kernels  86.5 us (98%)
  local copies, waits for them, and re-layouts  1.32 us (2%)
    pallas_call x1, Pallas kernels, per_device(): pl.pallas_call(kernel, out_shape=jax.ShapeDtypeStruct((64, 64, 256), BF),...  86.5 us

profile of v4, /device:TPU:1, one launch (start us, length us, event | category | flops | bytes accessed | tf_op | source)
XLA Modules:
  0.0 87.8 jit_solution(150209543654209807)
XLA Ops:
  0.0 86.5 %block.1 = bf16[64,64,256]{2,1,0:T(8,128)(2,1)S(1)} custom-call(bf16[32,128,256]{2,1,0:T(8,128)(2,1)} %latent_hbm.1, bf16[256,1024]{1,0:T(8,128)(2,1)} %w_expand_hbm.1, bf16[3,3,1024]{2,1,0:T(4,128)(2,1)} %taps_hbm.1, bf16[64,1024]{1,0:T(8,128)(2,1)} %bitcast.4, bf16[64,1024]{1,0:T(8,128)(2,1)} %up_hbm.1, bf16[1024,256]{1,0:T(8,128)(2,1)} %w_project_hbm.1, ...), custom_call_target="tpu_custom_call" | custom-call | tf_op jit(solution)/shard_map/block/pallas_call | solution.py:410
  86.5 1.3 %copy.14 = bf16[32,128,256]{2,1,0:T(8,128)(2,1)} copy(bf16[32,128,256]{2,1,0:T(8,128)(2,1)S(1)} %bitcast.3) | data formatting | bytes 4194304

commit v5 on v4

--- a/solution.py
+++ b/solution.py
@@ -247,7 +247,7 @@
     loads[3].wait()
     lax.fori_loop(0, 32 // EXPAND_ROWS, expand, 0)
     for copy in copies:
-        copy.wait()
+        copy.wait_recv()
     zero = jnp.zeros((), BF)
     edge_rows = []
     for i, (halo, inside) in enumerate(((halo_t, row > 0), (halo_b, row < ROWS - 1))):
@@ -324,7 +324,7 @@
         src_ref=ar2.at[core], dst_ref=ar2.at[core], send_sem=ar_send.at[1], recv_sem=ar_recv.at[1],
         device_id=(g * 2 + 1 - core, col), device_id_type=MESH)
     sibling.start()
-    sibling.wait()
+    sibling.wait_recv()
     mean = jnp.sum(ar2[...], axis=0) * (0.5 / (512 * 1024))
     squeeze = jnp.concatenate([mean[i : i + 1, :] for i in range(8)], axis=1)
     squeeze = jnp.broadcast_to(squeeze, (8, 1024))
@@ -384,10 +384,12 @@
 
     lax.fori_loop(0, BANDS, finish, 0)
     pltpu.make_async_copy(rest, rest, ar_send.at[0]).wait()
+    for copy in copies + [sibling]:
+        copy.wait_send()
 
 
 EXPAND_ROWS = 8
-DEPTH_ROWS = 4
+DEPTH_ROWS = 8
 
 
 def hops(offset):

time: 87.9 us -> 87.2 us (level)
  no operation moved by 1% of the time
where the time goes in v5:
time: 87.2 us; the launch traced here: 87.1 us
  Pallas kernels  85.8 us (98%)
  local copies, waits for them, and re-layouts  1.32 us (2%)
    pallas_call x1, Pallas kernels, per_device(): pl.pallas_call(kernel, out_shape=jax.ShapeDtypeStruct((64, 64, 256), BF),...  85.8 us

profile of v5, /device:TPU:1, one launch (start us, length us, event | category | flops | bytes accessed | tf_op | source)
XLA Modules:
  0.0 87.1 jit_solution(15102730586827388698)
XLA Ops:
  0.0 85.8 %block.1 = bf16[64,64,256]{2,1,0:T(8,128)(2,1)S(1)} custom-call(bf16[32,128,256]{2,1,0:T(8,128)(2,1)} %latent_hbm.1, bf16[256,1024]{1,0:T(8,128)(2,1)} %w_expand_hbm.1, bf16[3,3,1024]{2,1,0:T(4,128)(2,1)} %taps_hbm.1, bf16[64,1024]{1,0:T(8,128)(2,1)} %bitcast.4, bf16[64,1024]{1,0:T(8,128)(2,1)} %up_hbm.1, bf16[1024,256]{1,0:T(8,128)(2,1)} %w_project_hbm.1, ...), custom_call_target="tpu_custom_call" | custom-call | tf_op jit(solution)/shard_map/block/pallas_call | solution.py:412
  85.8 1.3 %copy.14 = bf16[32,128,256]{2,1,0:T(8,128)(2,1)} copy(bf16[32,128,256]{2,1,0:T(8,128)(2,1)S(1)} %bitcast.3) | data formatting | bytes 4194304
